TPU v7x, 32 devices: a whole 2x2x4 slice. The times are simulated.
32 devices in a mesh: gx: 8 (over z, y), gy: 4 (over x, core).
Axes of the slice: x: 2, y: 2, z: 4, core: 2. Of those that a mesh axis runs over, the one named last changes fastest.
Arguments:
- base_scores: float32 [12, 256, 64, 128], P(None, 'gx', 'gy'), may hold values from -6 to 6
- section_scores: float32 [12, 256, 64, 128], P(None, 'gx', 'gy'), may hold values from -6 to 6
- velocity: float32 [3, 256, 64, 128], P(None, 'gx', 'gy'), may hold values from -3 to 3
- diffusivity: float32 [256, 64, 128], P('gx', 'gy'), may hold values from 0.03 to 0.3
- w_first: bfloat16 [256, 12], replicated, may hold values from -1.75 to 1.75
- b_first: float32 [256], replicated, may hold values from -3 to 3
- w_second: bfloat16 [256, 256], replicated, may hold values from -0.375 to 0.375
- b_second: float32 [256], replicated, may hold values from -3 to 3
- w_third: bfloat16 [12, 256], replicated, may hold values from -0.375 to 0.375
- b_third: float32 [12], replicated, may hold values from -3 to 3
- loadings: bfloat16 [12, 300], replicated, may hold values from -0.375 to 0.375
- parcel_species: bfloat16 [1024, 300, 128], P(('gx', 'gy')), may hold values from -6 to 6
- parcel_owner: int32 [1024, 1], P(('gx', 'gy')), may hold values from 0 to 3; in each aligned block of 32 rows (0 to 31, 32 to 63, ...) at most 16 rows name the same one
- parcel_block: int32 [1024], P(('gx', 'gy')), may hold values from 0 to 31
Outputs:
- new_scores: float32 [12, 256, 64, 128], P(None, 'gx', 'gy')
Inputs may be any that keep to these rules, and one draw needn't show every extreme that they name: `parcel_owner`: among the 32 parcel blocks of one device, no tile y index is named by more than 16 of them, and in every draw some device's blocks name one index exactly 16 times.
All inputs are finite; a program needn't handle non-finite values.
Results may differ from a plain program's by a relative error of at most 0.0003.
Values sent between devices are 32-bit elements; how exact they have to be, the bound alone decides.
No kernel may reach another device: no remote copies, remote signals or barrier semaphores. Data moves between devices by JAX's collectives and lax.ppermute only.
A program may use at most 64 MiB of HBM per device.

v0:
```python
import math

import jax
import jax.numpy as jnp
from jax import lax
from jax.sharding import PartitionSpec as P

SB = 32


dt_step = 0.25


def with_halo(block, sides, width):
    for axis, dim in sides:
        count = lax.axis_size(axis)
        forward = [(i, i + 1) for i in range(count - 1)]
        backward = [(target, source) for source, target in forward]
        low = lax.ppermute(
            lax.slice_in_dim(block, block.shape[dim] - width, None, axis=dim), axis, forward
        )
        high = lax.ppermute(lax.slice_in_dim(block, 0, width, axis=dim), axis, backward)
        block = jnp.concatenate([low, block, high], axis=dim)
    return block


def regress(block, w_first, b_first, w_second, b_second, w_third, b_third):
    inputs = block.astype(jnp.bfloat16)
    first = jnp.tanh(
        jnp.dot(w_first, inputs, preferred_element_type=jnp.float32) + b_first[:, None]
    ).astype(jnp.bfloat16)
    second = jnp.tanh(
        jnp.dot(w_second, first, preferred_element_type=jnp.float32) + b_second[:, None]
    ).astype(jnp.bfloat16)
    return jnp.dot(w_third, second, preferred_element_type=jnp.float32) + b_third[:, None]


def sources(flat, weights):
    comps, count = flat.shape
    width = math.gcd(count, 4096)
    blocks = flat.reshape(comps, count // width, width).transpose(1, 0, 2)
    result = lax.map(lambda piece: regress(piece, *weights), blocks)
    return result.transpose(1, 0, 2).reshape(comps, count)


def transport_rate(
    center, plus_x, minus_x, plus_y, minus_y, plus_z, minus_z, velocity, diffusivity
):
    drift = (
        velocity[0] * (plus_x - minus_x)
        + velocity[1] * (plus_y - minus_y)
        + velocity[2] * (plus_z - minus_z)
    )
    spread = plus_x + minus_x + plus_y + minus_y + plus_z + minus_z - 6.0 * center
    return diffusivity * spread - 0.5 * drift


def shards(
    base_scores,
    section_scores,
    velocity,
    diffusivity,
    w_first,
    b_first,
    w_second,
    b_second,
    w_third,
    b_third,
    loadings,
    parcel_species,
    parcel_owner,
    parcel_block,
):
    comps, rows_x, rows_y, depth = section_scores.shape
    padded = with_halo(section_scores, (("gx", 1), ("gy", 2)), 1)
    plus_x = padded[:, 2:, 1:-1]
    minus_x = padded[:, :-2, 1:-1]
    plus_y = padded[:, 1:-1, 2:]
    minus_y = padded[:, 1:-1, :-2]
    along_z = jnp.pad(section_scores, ((0, 0), (0, 0), (0, 0), (1, 1)))
    transport = transport_rate(
        section_scores,
        plus_x,
        minus_x,
        plus_y,
        minus_y,
        along_z[..., 2:],
        along_z[..., :-2],
        velocity,
        diffusivity,
    )
    weights = (w_first, b_first, w_second, b_second, w_third, b_third)
    chemistry = sources(section_scores.reshape(comps, -1), weights).reshape(section_scores.shape)
    blocks_here = parcel_species.shape[0]
    block_cells = parcel_species.shape[2]
    projected = jnp.einsum(
        "ks,psc->pkc", loadings, parcel_species, preferred_element_type=jnp.float32
    ).astype(jnp.bfloat16)
    projected = projected.reshape(blocks_here, comps * block_cells)
    owner = parcel_owner[:, 0]
    tiles_y = lax.axis_size("gy")
    capacity = max(2, 2 * blocks_here // tiles_y)
    hits = (owner[:, None] == jnp.arange(tiles_y, dtype=jnp.int32)[None, :]).astype(jnp.int32)
    ranks = jnp.sum(jnp.cumsum(hits, axis=0) * hits, axis=1) - 1
    slot_ids = owner * capacity + ranks
    chosen = slot_ids[None, :] == jnp.arange(tiles_y * capacity, dtype=jnp.int32)[:, None]
    values = jnp.dot(chosen.astype(jnp.bfloat16), projected, preferred_element_type=jnp.float32)
    tags = jnp.sum(jnp.where(chosen, parcel_block[None, :] + 1, 0), axis=1)
    got_values, got_tags = (
        lax.all_to_all(values, "gy", split_axis=0, concat_axis=0, tiled=True),
        lax.all_to_all(tags, "gy", split_axis=0, concat_axis=0, tiled=True),
    )
    placing = (got_tags[None, :] - 1 == jnp.arange(SB, dtype=jnp.int32)[:, None]).astype(
        jnp.float32
    )
    mine = jnp.dot(
        placing, got_values, preferred_element_type=jnp.float32, precision=lax.Precision.HIGHEST
    )
    spray = mine.reshape(SB, comps, block_cells).transpose(1, 0, 2).reshape(comps, SB * block_cells)
    cells = rows_x * rows_y * depth
    spray = jnp.pad(spray, ((0, 0), (0, cells - SB * block_cells))).reshape(section_scores.shape)
    rate = transport + chemistry + spray
    return 0.75 * base_scores + 0.25 * (section_scores + dt_step * rate)


def solution(mesh):
    placed = (
        P(None, "gx", "gy", None),
        P(None, "gx", "gy", None),
        P(None, "gx", "gy", None),
        P("gx", "gy", None),
        P(),
        P(),
        P(),
        P(),
        P(),
        P(),
        P(),
        P(("gx", "gy"), None, None),
        P(("gx", "gy"), None),
        P(("gx", "gy")),
    )
    return jax.shard_map(
        shards, mesh=mesh, in_specs=placed, out_specs=P(None, "gx", "gy", None), check_vma=False
    )
```

profile of v0, /device:TPU:25, one launch (start us, length us, event | category | flops | bytes accessed | tf_op | source)
XLA Modules:
  0.0 160.6 jit_solution(15554967766689954134)
XLA Ops:
  0.0 0.7 fusion.22
  0.8 0.8 select_reduce_fusion.1
  1.6 0.7 add_add_fusion
  2.4 0.7 all_to_all.12
  3.1 3.9 %all-to-all-start = ((s32[4,16,1]{1,2,0:T(1,128)}), s32[4,16,1]{1,2,0:T(1,128)S(1)}, u32[]{:S(2)}, u32[]{:S(2)}) async-start(s32[4,16,1]{1,2,0:T(1,128)} %bitcast.9), calls=%async_computation | async-start | bytes 4096 | tf_op jit(solution)/shard_map/all_to_all | solution.py:111
  6.9 1.6 %fusion.28 = (f32[12,1,16,128]{3,2,1,0:T(8,128)}, f32[12,1,16,128]{3,2,1,0:T(8,128)}) fusion(f32[12,32,16,128]{3,2,1,0:T(8,128)} %param.17), kind=kLoop, calls=%fused_computation.50 | loop fusion | bytes 393216 | tf_op jit(solution)/shard_map/slice | solution.py:22
  8.6 3.1 %collective-permute-start.1 = (f32[12,1,16,128]{3,2,1,0:T(8,128)}, f32[12,1,16,128]{3,2,1,0:T(8,128)}, u32[]{:S(2)}, u32[]{:S(2)}) collective-permute-start(f32[12,1,16,128]{3,2,1,0:T(8,128)} %get-tuple-element.110), channel_id=1, source_target_pairs={{0,4},{4,8},{8,12},{12,16},{16,20},{20,24},{24,28},{1,5},{5,9},{9,... | collective-permute-start | bytes 294920 | tf_op jit(solution)/shard_map/ppermute | solution.py:19
  11.7 3.0 %collective-permute-start = (f32[12,1,16,128]{3,2,1,0:T(8,128)}, f32[12,1,16,128]{3,2,1,0:T(8,128)}, u32[]{:S(2)}, u32[]{:S(2)}) collective-permute-start(f32[12,1,16,128]{3,2,1,0:T(8,128)} %get-tuple-element.109), channel_id=1, source_target_pairs={{4,0},{8,4},{12,8},{16,12},{20,16},{24,20},{28,24},{5,1},{9,5},{13... | collective-permute-start | bytes 294920 | tf_op jit(solution)/shard_map/ppermute | solution.py:22
  14.9 3.0 %reshape_reshape.6 = bf16[12,16,4096]{2,1,0:T(8,128)(2,1)S(1)} reshape(f32[12,32,16,128]{3,2,1,0:T(8,128)} %param.17) | data formatting | bytes 4718592 | tf_op jit(solution)/shard_map/reshape;reshape | solution.py:41
  17.8 2.5 %fusion.13 = bf16[32,12,128]{2,1,0:T(8,128)(2,1)S(1)} fusion(bf16[32,300,128]{2,0,1:T(8,128)(2,1)} %param.27, bf16[12,300]{1,0:T(8,128)(2,1)S(1)} %copy-done), kind=kOutput, calls=%fused_computation.23 | convolution fusion | flops 29540352 | bytes 2563104 | tf_op jit(solution)/shard_map/ks,psc->pkc/dot_general | solution.py:96
  20.5 96.8 %while.10 = (s32[]{:T(128)}, f32[16,12,4096]{2,1,0:T(8,128)}, bf16[16,12,4096]{2,0,1:T(8,128)(2,1)S(1)}, bf16[256,12]{0,1:T(8,128)(2,1)S(1)}, f32[256]{0:T(256)S...) while((s32[]{:T(128)}, f32[16,12,4096]{2,1,0:T(8,128)}, ...), condition=%wide.region_1.2_spmd, body=%wide.region_0.1_spmd.sunk | while | flops 591446016 | bytes 4896933 | solution.py:42
  20.7 2.1 %fusion.46 = bf16[4096,256]{1,0:T(8,128)(2,1)} fusion(bf16[256,12]{0,1:T(8,128)(2,1)S(1)} %get-tuple-element.194, f32[256]{0:T(256)S(1)} %get-tuple-element.195, bf16[1,12,4096]{2,0,1:T(2,128)(2,1)S(1)} %constant_dynamic-slice_fusion.2), kind=kOutput, calls=%fused_computation.4.clone.1 | convolution fusion | flops 27262976 | bytes 2202624 | tf_op jit(solution)/shard_map/while/body/eval_jaxpr/dot_general | solution.py:30
  22.8 3.7 %fusion.47 = f32[16,12,4096]{2,1,0:T(8,128)} fusion(f32[16,12,4096]{2,1,0:T(8,128)} %get-tuple-element.182, s32[]{:T(128)S(6)} %copy.80, bf16[12,256]{1,0:T(8,128)(2,1)S(1)} %get-tuple-element.198, bf16[4096,256]{1,0:T(8,128)(2,1)} %fusion.46, bf16[256,256]{1,0:T(8,128)(2,1)S(1)} %get-tuple-element.196, f32[256]{0:T(256)S(1)} %get-tuple-element.197, ...), kind=kOutput, calls=%fused_computation.8.clone.1 | convolution fusion | flops 564183040 | bytes 2497588 | tf_op jit(solution)/shard_map/while/body/eval_jaxpr/dot_general | solution.py:35
  26.7 2.1 %fusion.46 = bf16[4096,256]{1,0:T(8,128)(2,1)} fusion(bf16[256,12]{0,1:T(8,128)(2,1)S(1)} %get-tuple-element.194, f32[256]{0:T(256)S(1)} %get-tuple-element.195, bf16[1,12,4096]{2,0,1:T(2,128)(2,1)S(1)} %constant_dynamic-slice_fusion.2), kind=kOutput, calls=%fused_computation.4.clone.1 | convolution fusion | flops 27262976 | bytes 2202624 | tf_op jit(solution)/shard_map/while/body/eval_jaxpr/dot_general | solution.py:30
  28.9 3.7 %fusion.47 = f32[16,12,4096]{2,1,0:T(8,128)} fusion(f32[16,12,4096]{2,1,0:T(8,128)} %get-tuple-element.182, s32[]{:T(128)S(6)} %copy.80, bf16[12,256]{1,0:T(8,128)(2,1)S(1)} %get-tuple-element.198, bf16[4096,256]{1,0:T(8,128)(2,1)} %fusion.46, bf16[256,256]{1,0:T(8,128)(2,1)S(1)} %get-tuple-element.196, f32[256]{0:T(256)S(1)} %get-tuple-element.197, ...), kind=kOutput, calls=%fused_computation.8.clone.1 | convolution fusion | flops 564183040 | bytes 2497588 | tf_op jit(solution)/shard_map/while/body/eval_jaxpr/dot_general | solution.py:35
  32.8 2.1 %fusion.46 = bf16[4096,256]{1,0:T(8,128)(2,1)} fusion(bf16[256,12]{0,1:T(8,128)(2,1)S(1)} %get-tuple-element.194, f32[256]{0:T(256)S(1)} %get-tuple-element.195, bf16[1,12,4096]{2,0,1:T(2,128)(2,1)S(1)} %constant_dynamic-slice_fusion.2), kind=kOutput, calls=%fused_computation.4.clone.1 | convolution fusion | flops 27262976 | bytes 2202624 | tf_op jit(solution)/shard_map/while/body/eval_jaxpr/dot_general | solution.py:30
  34.9 3.7 %fusion.47 = f32[16,12,4096]{2,1,0:T(8,128)} fusion(f32[16,12,4096]{2,1,0:T(8,128)} %get-tuple-element.182, s32[]{:T(128)S(6)} %copy.80, bf16[12,256]{1,0:T(8,128)(2,1)S(1)} %get-tuple-element.198, bf16[4096,256]{1,0:T(8,128)(2,1)} %fusion.46, bf16[256,256]{1,0:T(8,128)(2,1)S(1)} %get-tuple-element.196, f32[256]{0:T(256)S(1)} %get-tuple-element.197, ...), kind=kOutput, calls=%fused_computation.8.clone.1 | convolution fusion | flops 564183040 | bytes 2497588 | tf_op jit(solution)/shard_map/while/body/eval_jaxpr/dot_general | solution.py:35
  38.8 2.1 %fusion.46 = bf16[4096,256]{1,0:T(8,128)(2,1)} fusion(bf16[256,12]{0,1:T(8,128)(2,1)S(1)} %get-tuple-element.194, f32[256]{0:T(256)S(1)} %get-tuple-element.195, bf16[1,12,4096]{2,0,1:T(2,128)(2,1)S(1)} %constant_dynamic-slice_fusion.2), kind=kOutput, calls=%fused_computation.4.clone.1 | convolution fusion | flops 27262976 | bytes 2202624 | tf_op jit(solution)/shard_map/while/body/eval_jaxpr/dot_general | solution.py:30
  40.9 3.7 %fusion.47 = f32[16,12,4096]{2,1,0:T(8,128)} fusion(f32[16,12,4096]{2,1,0:T(8,128)} %get-tuple-element.182, s32[]{:T(128)S(6)} %copy.80, bf16[12,256]{1,0:T(8,128)(2,1)S(1)} %get-tuple-element.198, bf16[4096,256]{1,0:T(8,128)(2,1)} %fusion.46, bf16[256,256]{1,0:T(8,128)(2,1)S(1)} %get-tuple-element.196, f32[256]{0:T(256)S(1)} %get-tuple-element.197, ...), kind=kOutput, calls=%fused_computation.8.clone.1 | convolution fusion | flops 564183040 | bytes 2497588 | tf_op jit(solution)/shard_map/while/body/eval_jaxpr/dot_general | solution.py:35
  44.9 2.1 %fusion.46 = bf16[4096,256]{1,0:T(8,128)(2,1)} fusion(bf16[256,12]{0,1:T(8,128)(2,1)S(1)} %get-tuple-element.194, f32[256]{0:T(256)S(1)} %get-tuple-element.195, bf16[1,12,4096]{2,0,1:T(2,128)(2,1)S(1)} %constant_dynamic-slice_fusion.2), kind=kOutput, calls=%fused_computation.4.clone.1 | convolution fusion | flops 27262976 | bytes 2202624 | tf_op jit(solution)/shard_map/while/body/eval_jaxpr/dot_general | solution.py:30
  47.0 3.7 %fusion.47 = f32[16,12,4096]{2,1,0:T(8,128)} fusion(f32[16,12,4096]{2,1,0:T(8,128)} %get-tuple-element.182, s32[]{:T(128)S(6)} %copy.80, bf16[12,256]{1,0:T(8,128)(2,1)S(1)} %get-tuple-element.198, bf16[4096,256]{1,0:T(8,128)(2,1)} %fusion.46, bf16[256,256]{1,0:T(8,128)(2,1)S(1)} %get-tuple-element.196, f32[256]{0:T(256)S(1)} %get-tuple-element.197, ...), kind=kOutput, calls=%fused_computation.8.clone.1 | convolution fusion | flops 564183040 | bytes 2497588 | tf_op jit(solution)/shard_map/while/body/eval_jaxpr/dot_general | solution.py:35
  50.9 2.1 %fusion.46 = bf16[4096,256]{1,0:T(8,128)(2,1)} fusion(bf16[256,12]{0,1:T(8,128)(2,1)S(1)} %get-tuple-element.194, f32[256]{0:T(256)S(1)} %get-tuple-element.195, bf16[1,12,4096]{2,0,1:T(2,128)(2,1)S(1)} %constant_dynamic-slice_fusion.2), kind=kOutput, calls=%fused_computation.4.clone.1 | convolution fusion | flops 27262976 | bytes 2202624 | tf_op jit(solution)/shard_map/while/body/eval_jaxpr/dot_general | solution.py:30
  53.1 3.7 %fusion.47 = f32[16,12,4096]{2,1,0:T(8,128)} fusion(f32[16,12,4096]{2,1,0:T(8,128)} %get-tuple-element.182, s32[]{:T(128)S(6)} %copy.80, bf16[12,256]{1,0:T(8,128)(2,1)S(1)} %get-tuple-element.198, bf16[4096,256]{1,0:T(8,128)(2,1)} %fusion.46, bf16[256,256]{1,0:T(8,128)(2,1)S(1)} %get-tuple-element.196, f32[256]{0:T(256)S(1)} %get-tuple-element.197, ...), kind=kOutput, calls=%fused_computation.8.clone.1 | convolution fusion | flops 564183040 | bytes 2497588 | tf_op jit(solution)/shard_map/while/body/eval_jaxpr/dot_general | solution.py:35
  57.0 2.1 %fusion.46 = bf16[4096,256]{1,0:T(8,128)(2,1)} fusion(bf16[256,12]{0,1:T(8,128)(2,1)S(1)} %get-tuple-element.194, f32[256]{0:T(256)S(1)} %get-tuple-element.195, bf16[1,12,4096]{2,0,1:T(2,128)(2,1)S(1)} %constant_dynamic-slice_fusion.2), kind=kOutput, calls=%fused_computation.4.clone.1 | convolution fusion | flops 27262976 | bytes 2202624 | tf_op jit(solution)/shard_map/while/body/eval_jaxpr/dot_general | solution.py:30
  59.1 3.7 %fusion.47 = f32[16,12,4096]{2,1,0:T(8,128)} fusion(f32[16,12,4096]{2,1,0:T(8,128)} %get-tuple-element.182, s32[]{:T(128)S(6)} %copy.80, bf16[12,256]{1,0:T(8,128)(2,1)S(1)} %get-tuple-element.198, bf16[4096,256]{1,0:T(8,128)(2,1)} %fusion.46, bf16[256,256]{1,0:T(8,128)(2,1)S(1)} %get-tuple-element.196, f32[256]{0:T(256)S(1)} %get-tuple-element.197, ...), kind=kOutput, calls=%fused_computation.8.clone.1 | convolution fusion | flops 564183040 | bytes 2497588 | tf_op jit(solution)/shard_map/while/body/eval_jaxpr/dot_general | solution.py:35
  63.0 2.1 %fusion.46 = bf16[4096,256]{1,0:T(8,128)(2,1)} fusion(bf16[256,12]{0,1:T(8,128)(2,1)S(1)} %get-tuple-element.194, f32[256]{0:T(256)S(1)} %get-tuple-element.195, bf16[1,12,4096]{2,0,1:T(2,128)(2,1)S(1)} %constant_dynamic-slice_fusion.2), kind=kOutput, calls=%fused_computation.4.clone.1 | convolution fusion | flops 27262976 | bytes 2202624 | tf_op jit(solution)/shard_map/while/body/eval_jaxpr/dot_general | solution.py:30
  65.2 3.7 %fusion.47 = f32[16,12,4096]{2,1,0:T(8,128)} fusion(f32[16,12,4096]{2,1,0:T(8,128)} %get-tuple-element.182, s32[]{:T(128)S(6)} %copy.80, bf16[12,256]{1,0:T(8,128)(2,1)S(1)} %get-tuple-element.198, bf16[4096,256]{1,0:T(8,128)(2,1)} %fusion.46, bf16[256,256]{1,0:T(8,128)(2,1)S(1)} %get-tuple-element.196, f32[256]{0:T(256)S(1)} %get-tuple-element.197, ...), kind=kOutput, calls=%fused_computation.8.clone.1 | convolution fusion | flops 564183040 | bytes 2497588 | tf_op jit(solution)/shard_map/while/body/eval_jaxpr/dot_general | solution.py:35
  69.1 2.1 %fusion.46 = bf16[4096,256]{1,0:T(8,128)(2,1)} fusion(bf16[256,12]{0,1:T(8,128)(2,1)S(1)} %get-tuple-element.194, f32[256]{0:T(256)S(1)} %get-tuple-element.195, bf16[1,12,4096]{2,0,1:T(2,128)(2,1)S(1)} %constant_dynamic-slice_fusion.2), kind=kOutput, calls=%fused_computation.4.clone.1 | convolution fusion | flops 27262976 | bytes 2202624 | tf_op jit(solution)/shard_map/while/body/eval_jaxpr/dot_general | solution.py:30
  71.2 3.7 %fusion.47 = f32[16,12,4096]{2,1,0:T(8,128)} fusion(f32[16,12,4096]{2,1,0:T(8,128)} %get-tuple-element.182, s32[]{:T(128)S(6)} %copy.80, bf16[12,256]{1,0:T(8,128)(2,1)S(1)} %get-tuple-element.198, bf16[4096,256]{1,0:T(8,128)(2,1)} %fusion.46, bf16[256,256]{1,0:T(8,128)(2,1)S(1)} %get-tuple-element.196, f32[256]{0:T(256)S(1)} %get-tuple-element.197, ...), kind=kOutput, calls=%fused_computation.8.clone.1 | convolution fusion | flops 564183040 | bytes 2497588 | tf_op jit(solution)/shard_map/while/body/eval_jaxpr/dot_general | solution.py:35
  75.2 2.1 %fusion.46 = bf16[4096,256]{1,0:T(8,128)(2,1)} fusion(bf16[256,12]{0,1:T(8,128)(2,1)S(1)} %get-tuple-element.194, f32[256]{0:T(256)S(1)} %get-tuple-element.195, bf16[1,12,4096]{2,0,1:T(2,128)(2,1)S(1)} %constant_dynamic-slice_fusion.2), kind=kOutput, calls=%fused_computation.4.clone.1 | convolution fusion | flops 27262976 | bytes 2202624 | tf_op jit(solution)/shard_map/while/body/eval_jaxpr/dot_general | solution.py:30
  77.3 3.7 %fusion.47 = f32[16,12,4096]{2,1,0:T(8,128)} fusion(f32[16,12,4096]{2,1,0:T(8,128)} %get-tuple-element.182, s32[]{:T(128)S(6)} %copy.80, bf16[12,256]{1,0:T(8,128)(2,1)S(1)} %get-tuple-element.198, bf16[4096,256]{1,0:T(8,128)(2,1)} %fusion.46, bf16[256,256]{1,0:T(8,128)(2,1)S(1)} %get-tuple-element.196, f32[256]{0:T(256)S(1)} %get-tuple-element.197, ...), kind=kOutput, calls=%fused_computation.8.clone.1 | convolution fusion | flops 564183040 | bytes 2497588 | tf_op jit(solution)/shard_map/while/body/eval_jaxpr/dot_general | solution.py:35
  81.2 2.1 %fusion.46 = bf16[4096,256]{1,0:T(8,128)(2,1)} fusion(bf16[256,12]{0,1:T(8,128)(2,1)S(1)} %get-tuple-element.194, f32[256]{0:T(256)S(1)} %get-tuple-element.195, bf16[1,12,4096]{2,0,1:T(2,128)(2,1)S(1)} %constant_dynamic-slice_fusion.2), kind=kOutput, calls=%fused_computation.4.clone.1 | convolution fusion | flops 27262976 | bytes 2202624 | tf_op jit(solution)/shard_map/while/body/eval_jaxpr/dot_general | solution.py:30
  83.3 3.7 %fusion.47 = f32[16,12,4096]{2,1,0:T(8,128)} fusion(f32[16,12,4096]{2,1,0:T(8,128)} %get-tuple-element.182, s32[]{:T(128)S(6)} %copy.80, bf16[12,256]{1,0:T(8,128)(2,1)S(1)} %get-tuple-element.198, bf16[4096,256]{1,0:T(8,128)(2,1)} %fusion.46, bf16[256,256]{1,0:T(8,128)(2,1)S(1)} %get-tuple-element.196, f32[256]{0:T(256)S(1)} %get-tuple-element.197, ...), kind=kOutput, calls=%fused_computation.8.clone.1 | convolution fusion | flops 564183040 | bytes 2497588 | tf_op jit(solution)/shard_map/while/body/eval_jaxpr/dot_general | solution.py:35
  87.3 2.1 %fusion.46 = bf16[4096,256]{1,0:T(8,128)(2,1)} fusion(bf16[256,12]{0,1:T(8,128)(2,1)S(1)} %get-tuple-element.194, f32[256]{0:T(256)S(1)} %get-tuple-element.195, bf16[1,12,4096]{2,0,1:T(2,128)(2,1)S(1)} %constant_dynamic-slice_fusion.2), kind=kOutput, calls=%fused_computation.4.clone.1 | convolution fusion | flops 27262976 | bytes 2202624 | tf_op jit(solution)/shard_map/while/body/eval_jaxpr/dot_general | solution.py:30
  89.4 3.7 %fusion.47 = f32[16,12,4096]{2,1,0:T(8,128)} fusion(f32[16,12,4096]{2,1,0:T(8,128)} %get-tuple-element.182, s32[]{:T(128)S(6)} %copy.80, bf16[12,256]{1,0:T(8,128)(2,1)S(1)} %get-tuple-element.198, bf16[4096,256]{1,0:T(8,128)(2,1)} %fusion.46, bf16[256,256]{1,0:T(8,128)(2,1)S(1)} %get-tuple-element.196, f32[256]{0:T(256)S(1)} %get-tuple-element.197, ...), kind=kOutput, calls=%fused_computation.8.clone.1 | convolution fusion | flops 564183040 | bytes 2497588 | tf_op jit(solution)/shard_map/while/body/eval_jaxpr/dot_general | solution.py:35
  93.3 2.1 %fusion.46 = bf16[4096,256]{1,0:T(8,128)(2,1)} fusion(bf16[256,12]{0,1:T(8,128)(2,1)S(1)} %get-tuple-element.194, f32[256]{0:T(256)S(1)} %get-tuple-element.195, bf16[1,12,4096]{2,0,1:T(2,128)(2,1)S(1)} %constant_dynamic-slice_fusion.2), kind=kOutput, calls=%fused_computation.4.clone.1 | convolution fusion | flops 27262976 | bytes 2202624 | tf_op jit(solution)/shard_map/while/body/eval_jaxpr/dot_general | solution.py:30
  95.5 3.7 %fusion.47 = f32[16,12,4096]{2,1,0:T(8,128)} fusion(f32[16,12,4096]{2,1,0:T(8,128)} %get-tuple-element.182, s32[]{:T(128)S(6)} %copy.80, bf16[12,256]{1,0:T(8,128)(2,1)S(1)} %get-tuple-element.198, bf16[4096,256]{1,0:T(8,128)(2,1)} %fusion.46, bf16[256,256]{1,0:T(8,128)(2,1)S(1)} %get-tuple-element.196, f32[256]{0:T(256)S(1)} %get-tuple-element.197, ...), kind=kOutput, calls=%fused_computation.8.clone.1 | convolution fusion | flops 564183040 | bytes 2497588 | tf_op jit(solution)/shard_map/while/body/eval_jaxpr/dot_general | solution.py:35
  99.4 2.1 %fusion.46 = bf16[4096,256]{1,0:T(8,128)(2,1)} fusion(bf16[256,12]{0,1:T(8,128)(2,1)S(1)} %get-tuple-element.194, f32[256]{0:T(256)S(1)} %get-tuple-element.195, bf16[1,12,4096]{2,0,1:T(2,128)(2,1)S(1)} %constant_dynamic-slice_fusion.2), kind=kOutput, calls=%fused_computation.4.clone.1 | convolution fusion | flops 27262976 | bytes 2202624 | tf_op jit(solution)/shard_map/while/body/eval_jaxpr/dot_general | solution.py:30
  101.5 3.7 %fusion.47 = f32[16,12,4096]{2,1,0:T(8,128)} fusion(f32[16,12,4096]{2,1,0:T(8,128)} %get-tuple-element.182, s32[]{:T(128)S(6)} %copy.80, bf16[12,256]{1,0:T(8,128)(2,1)S(1)} %get-tuple-element.198, bf16[4096,256]{1,0:T(8,128)(2,1)} %fusion.46, bf16[256,256]{1,0:T(8,128)(2,1)S(1)} %get-tuple-element.196, f32[256]{0:T(256)S(1)} %get-tuple-element.197, ...), kind=kOutput, calls=%fused_computation.8.clone.1 | convolution fusion | flops 564183040 | bytes 2497588 | tf_op jit(solution)/shard_map/while/body/eval_jaxpr/dot_general | solution.py:35
  105.4 2.1 %fusion.46 = bf16[4096,256]{1,0:T(8,128)(2,1)} fusion(bf16[256,12]{0,1:T(8,128)(2,1)S(1)} %get-tuple-element.194, f32[256]{0:T(256)S(1)} %get-tuple-element.195, bf16[1,12,4096]{2,0,1:T(2,128)(2,1)S(1)} %constant_dynamic-slice_fusion.2), kind=kOutput, calls=%fused_computation.4.clone.1 | convolution fusion | flops 27262976 | bytes 2202624 | tf_op jit(solution)/shard_map/while/body/eval_jaxpr/dot_general | solution.py:30
  107.5 3.7 %fusion.47 = f32[16,12,4096]{2,1,0:T(8,128)} fusion(f32[16,12,4096]{2,1,0:T(8,128)} %get-tuple-element.182, s32[]{:T(128)S(6)} %copy.80, bf16[12,256]{1,0:T(8,128)(2,1)S(1)} %get-tuple-element.198, bf16[4096,256]{1,0:T(8,128)(2,1)} %fusion.46, bf16[256,256]{1,0:T(8,128)(2,1)S(1)} %get-tuple-element.196, f32[256]{0:T(256)S(1)} %get-tuple-element.197, ...), kind=kOutput, calls=%fused_computation.8.clone.1 | convolution fusion | flops 564183040 | bytes 2497588 | tf_op jit(solution)/shard_map/while/body/eval_jaxpr/dot_general | solution.py:35
  111.5 2.1 %fusion.46 = bf16[4096,256]{1,0:T(8,128)(2,1)} fusion(bf16[256,12]{0,1:T(8,128)(2,1)S(1)} %get-tuple-element.194, f32[256]{0:T(256)S(1)} %get-tuple-element.195, bf16[1,12,4096]{2,0,1:T(2,128)(2,1)S(1)} %constant_dynamic-slice_fusion.2), kind=kOutput, calls=%fused_computation.4.clone.1 | convolution fusion | flops 27262976 | bytes 2202624 | tf_op jit(solution)/shard_map/while/body/eval_jaxpr/dot_general | solution.py:30
  113.6 3.7 %fusion.47 = f32[16,12,4096]{2,1,0:T(8,128)} fusion(f32[16,12,4096]{2,1,0:T(8,128)} %get-tuple-element.182, s32[]{:T(128)S(6)} %copy.80, bf16[12,256]{1,0:T(8,128)(2,1)S(1)} %get-tuple-element.198, bf16[4096,256]{1,0:T(8,128)(2,1)} %fusion.46, bf16[256,256]{1,0:T(8,128)(2,1)S(1)} %get-tuple-element.196, f32[256]{0:T(256)S(1)} %get-tuple-element.197, ...), kind=kOutput, calls=%fused_computation.8.clone.1 | convolution fusion | flops 564183040 | bytes 2497588 | tf_op jit(solution)/shard_map/while/body/eval_jaxpr/dot_general | solution.py:35
  117.3 0.9 slice_bitcast_fusion.2
  118.2 1.0 fusion.18
  119.1 5.7 %copy.53 = f32[12,16,4096]{2,1,0:T(8,128)} copy(f32[12,16,4096]{2,0,1:T(8,128)} %bitcast.66) | data formatting | bytes 6291456 | tf_op jit(solution)/shard_map/transpose | solution.py:43
  124.8 4.7 %reshape_reshape.7 = f32[12,32,16,128]{3,2,1,0:T(8,128)} reshape(f32[12,16,4096]{2,1,0:T(8,128)} %copy.53) | data formatting | bytes 6291456 | tf_op jit(solution)/shard_map/reshape;reshape | solution.py:93
  129.6 0.6 copy-done.8
  130.1 4.0 %all-to-all-start.1 = ((f32[4,16,1536]{2,1,0:T(8,128)}), f32[4,16,1536]{2,1,0:T(8,128)S(1)}, u32[]{:S(2)}, u32[]{:S(2)}) async-start(f32[4,16,1536]{2,1,0:T(8,128)} %fusion.18), calls=%async_computation.1 | async-start | bytes 786432 | tf_op jit(solution)/shard_map/all_to_all | solution.py:110
  134.2 0.7 add_reduce_fusion
  134.9 0.6 sub.32
  135.4 0.9 constant_dynamic-update-slice_fusion.2
  136.4 0.3 constant_dynamic-update-slice_fusion.1
  136.7 0.9 constant_dynamic-update-slice_fusion
  137.6 1.7 %copy-done.3 = f32[12,34,16,128]{3,2,1,0:T(8,128)} copy-done((f32[12,34,16,128]{3,2,1,0:T(8,128)}, f32[12,34,16,128]{3,2,1,0:T(8,128)S(1)}, u32[]{:S(2)}) %copy-start.3) | copy-done | bytes 3342360
  139.6 0.7 copy.50
  140.3 3.5 %collective-permute-start.3 = (f32[12,34,1,128]{3,1,2,0:T(8,128)}, f32[12,34,1,128]{3,1,2,0:T(8,128)}, u32[]{:S(2)}, u32[]{:S(2)}) collective-permute-start(f32[12,34,1,128]{3,1,2,0:T(8,128)} %copy.50), channel_id=1, source_target_pairs={{0,1},{1,2},{2,3},{4,5},{5,6},{6,7},{8,9},{9,10},{10,11},{12,13},{... | collective-permute-start | bytes 626696 | tf_op jit(solution)/shard_map/ppermute | solution.py:19
  143.8 0.7 copy.48
  144.5 1.9 %collective-permute-start.2 = (f32[12,34,1,128]{3,1,2,0:T(8,128)}, f32[12,34,1,128]{3,1,2,0:T(8,128)}, u32[]{:S(2)}, u32[]{:S(2)}) collective-permute-start(f32[12,34,1,128]{3,1,2,0:T(8,128)} %copy.48), channel_id=1, source_target_pairs={{1,0},{2,1},{3,2},{5,4},{6,5},{7,6},{9,8},{10,9},{11,10},{13,12},{... | collective-permute-start | bytes 626696 | tf_op jit(solution)/shard_map/ppermute | solution.py:22
  147.2 0.8 copy.60
  148.3 2.1 %copy.51 = f32[12,34,1,128]{3,2,1,0:T(1,128)} copy(f32[12,34,1,128]{3,1,2,0:T(8,128)} %collective-permute-done.3) | data formatting | bytes 417792 | tf_op jit(solution)/shard_map/ppermute | solution.py:19
  150.4 2.0 %collective-permute-done.2 = f32[12,34,1,128]{3,1,2,0:T(8,128)} collective-permute-done((f32[12,34,1,128]{3,1,2,0:T(8,128)}, f32[12,34,1,128]{3,1,2,0:T(8,128)}, u32[]{:S(2)}, u32[]{:S(2)}) %collective-permute-start.2) | collective-permute-done | bytes 208928 | tf_op jit(solution)/shard_map/ppermute | solution.py:22
  152.4 1.9 %copy.49 = f32[12,34,1,128]{3,2,1,0:T(1,128)} copy(f32[12,34,1,128]{3,1,2,0:T(8,128)} %collective-permute-done.2) | data formatting | bytes 417792 | tf_op jit(solution)/shard_map/ppermute | solution.py:22
  154.2 6.3 %multiply_add_fusion = f32[12,32,16,128]{3,2,1,0:T(8,128)} fusion(f32[12,32,16,128]{3,2,1,0:T(8,128)S(1)} %copy-done.1, f32[12,32,16,128]{3,2,1,0:T(8,128)S(1)} %bitcast.65, f32[12,32,16,128]{3,2,1,0:T(8,128)S(1)} %copy-done.2, f32[12,34,16,128]{3,2,1,0:T(8,128)S(1)} %copy-done.4, f32[12,34,1,128]{3,2,1,0:T(1,128)} %copy.51, f32[12,34,1,128]{3,2,1,0:T(1,128)} %copy.49, ...), kind=kLoop, calls=%fused_computation.18 | loop fusion | flops 22806528 | bytes 20733952 | tf_op jit(solution)/shard_map/add | solution.py:123
  (62 shorter events, 5.1 us)
Async XLA Ops:
  0.0 17.8 %copy-start = (bf16[12,300]{1,0:T(8,128)(2,1)S(1)}, bf16[12,300]{1,0:T(8,128)(2,1)}, u32[]{:S(2)}) copy-start(bf16[12,300]{1,0:T(8,128)(2,1)} %param.26) | copy-start | bytes 21604
  3.1 126.5 %all-to-all-start = ((s32[4,16,1]{1,2,0:T(1,128)}), s32[4,16,1]{1,2,0:T(1,128)S(1)}, u32[]{:S(2)}, u32[]{:S(2)}) async-start(s32[4,16,1]{1,2,0:T(1,128)} %bitcast.9), calls=%async_computation | async-start | bytes 4096 | tf_op jit(solution)/shard_map/all_to_all | solution.py:111
  8.6 126.9 %collective-permute-start.1 = (f32[12,1,16,128]{3,2,1,0:T(8,128)}, f32[12,1,16,128]{3,2,1,0:T(8,128)}, u32[]{:S(2)}, u32[]{:S(2)}) collective-permute-start(f32[12,1,16,128]{3,2,1,0:T(8,128)} %get-tuple-element.110), channel_id=1, source_target_pairs={{0,4},{4,8},{8,12},{12,16},{16,20},{20,24},{24,28},{1,5},{5,9},{9,... | collective-permute-start | bytes 294920 | tf_op jit(solution)/shard_map/ppermute | solution.py:19
  11.7 124.9 %collective-permute-start = (f32[12,1,16,128]{3,2,1,0:T(8,128)}, f32[12,1,16,128]{3,2,1,0:T(8,128)}, u32[]{:S(2)}, u32[]{:S(2)}) collective-permute-start(f32[12,1,16,128]{3,2,1,0:T(8,128)} %get-tuple-element.109), channel_id=1, source_target_pairs={{4,0},{8,4},{12,8},{16,12},{20,16},{24,20},{28,24},{5,1},{9,5},{13... | collective-permute-start | bytes 294920 | tf_op jit(solution)/shard_map/ppermute | solution.py:22
  14.8 5.6 %copy-start.10 = (bf16[256,256]{1,0:T(8,128)(2,1)S(1)}, bf16[256,256]{1,0:T(8,128)(2,1)}, u32[]{:S(2)}) copy-start(bf16[256,256]{1,0:T(8,128)(2,1)} %param.22) | copy-start | bytes 393220
  14.8 5.6 %copy-start.11 = (bf16[256,12]{0,1:T(8,128)(2,1)S(1)}, bf16[256,12]{0,1:T(8,128)(2,1)}, u32[]{:S(2)}) copy-start(bf16[256,12]{0,1:T(8,128)(2,1)} %param.20) | copy-start | bytes 18436
  14.8 5.6 %copy-start.12 = (bf16[12,256]{1,0:T(8,128)(2,1)S(1)}, bf16[12,256]{1,0:T(8,128)(2,1)}, u32[]{:S(2)}) copy-start(bf16[12,256]{1,0:T(8,128)(2,1)} %param.24) | copy-start | bytes 18436
  14.8 5.6 %copy-start.13 = (f32[256]{0:T(256)S(1)}, f32[256]{0:T(256)}, u32[]{:S(2)}) copy-start(f32[256]{0:T(256)} %param.21) | copy-start | bytes 3076
  14.8 5.6 %copy-start.14 = (f32[256]{0:T(256)S(1)}, f32[256]{0:T(256)}, u32[]{:S(2)}) copy-start(f32[256]{0:T(256)} %param.23) | copy-start | bytes 3076
  14.9 5.6 %copy-start.15 = (f32[12]{0:T(128)S(1)}, f32[12]{0:T(128)}, u32[]{:S(2)}) copy-start(f32[12]{0:T(128)} %param.25) | copy-start | bytes 148
  20.4 96.8 %copy-start.7 = (f32[3,32,16,128]{3,2,1,0:T(8,128)S(1)}, f32[3,32,16,128]{3,2,1,0:T(8,128)}, u32[]{:S(2)}) copy-start(f32[3,32,16,128]{3,2,1,0:T(8,128)} %param.18) | copy-start | bytes 2359300
  124.8 11.5 %copy-start.1 = (f32[12,32,16,128]{3,2,1,0:T(8,128)S(1)}, f32[12,32,16,128]{3,2,1,0:T(8,128)}, u32[]{:S(2)}) copy-start(f32[12,32,16,128]{3,2,1,0:T(8,128)} %param.17) | copy-start | bytes 9437188
  129.6 0.6 copy-start.8
  130.1 16.3 %all-to-all-start.1 = ((f32[4,16,1536]{2,1,0:T(8,128)}), f32[4,16,1536]{2,1,0:T(8,128)S(1)}, u32[]{:S(2)}, u32[]{:S(2)}) async-start(f32[4,16,1536]{2,1,0:T(8,128)} %fusion.18), calls=%async_computation.1 | async-start | bytes 786432 | tf_op jit(solution)/shard_map/all_to_all | solution.py:110
  136.3 10.1 %copy-start.9 = (s32[64]{0:T(128)S(1)}, s32[64]{0:T(128)}, u32[]{:S(2)}) copy-start(s32[64]{0:T(128)} %sub.32) | copy-start | bytes 772
  137.6 1.7 %copy-start.3 = (f32[12,34,16,128]{3,2,1,0:T(8,128)}, f32[12,34,16,128]{3,2,1,0:T(8,128)S(1)}, u32[]{:S(2)}) copy-start(f32[12,34,16,128]{3,2,1,0:T(8,128)S(1)} %constant_dynamic-update-slice_fusion) | copy-start | bytes 10027012
  140.3 8.0 %collective-permute-start.3 = (f32[12,34,1,128]{3,1,2,0:T(8,128)}, f32[12,34,1,128]{3,1,2,0:T(8,128)}, u32[]{:S(2)}, u32[]{:S(2)}) collective-permute-start(f32[12,34,1,128]{3,1,2,0:T(8,128)} %copy.50), channel_id=1, source_target_pairs={{0,1},{1,2},{2,3},{4,5},{5,6},{6,7},{8,9},{9,10},{10,11},{12,13},{... | collective-permute-start | bytes 626696 | tf_op jit(solution)/shard_map/ppermute | solution.py:19
  144.5 7.8 %collective-permute-start.2 = (f32[12,34,1,128]{3,1,2,0:T(8,128)}, f32[12,34,1,128]{3,1,2,0:T(8,128)}, u32[]{:S(2)}, u32[]{:S(2)}) collective-permute-start(f32[12,34,1,128]{3,1,2,0:T(8,128)} %copy.48), channel_id=1, source_target_pairs={{1,0},{2,1},{3,2},{5,4},{6,5},{7,6},{9,8},{10,9},{11,10},{13,12},{... | collective-permute-start | bytes 626696 | tf_op jit(solution)/shard_map/ppermute | solution.py:22
  147.2 7.0 %copy-start.5 = (f32[12,32,16,128]{3,2,1,0:T(8,128)S(1)}, f32[12,32,16,128]{3,2,1,0:T(8,128)}, u32[]{:S(2)}) copy-start(f32[12,32,16,128]{3,2,1,0:T(8,128)} %param.16) | copy-start | bytes 9437188
  148.1 6.2 %copy-start.2 = (f32[12,32,16,128]{3,2,1,0:T(8,128)S(1)}, f32[12,32,16,128]{3,2,1,0:T(8,128)}, u32[]{:S(2)}) copy-start(f32[12,32,16,128]{3,2,1,0:T(8,128)} %reshape_reshape.7) | copy-start | bytes 9437188
  148.1 6.2 %copy-start.4 = (f32[12,34,16,128]{3,2,1,0:T(8,128)S(1)}, f32[12,34,16,128]{3,2,1,0:T(8,128)}, u32[]{:S(2)}) copy-start(f32[12,34,16,128]{3,2,1,0:T(8,128)} %copy-done.3) | copy-start | bytes 10027012
  148.1 6.2 %copy-start.6 = (f32[32,16,128]{2,1,0:T(8,128)S(1)}, f32[32,16,128]{2,1,0:T(8,128)}, u32[]{:S(2)}) copy-start(f32[32,16,128]{2,1,0:T(8,128)} %get-tuple-element.111) | copy-start | bytes 786436
where the time goes:
time: 162 us; the launch traced here: 161 us
  matrix products  96.9 us (60%)
  local copies, waits for them, and re-layouts  32.3 us (20%)
  starting transfers between devices  19.5 us (12%)
  other arithmetic  9.45 us (6%)
  waiting for transfers between devices  1.98 us (1%)
    dot_general x16, matrix products, regress(): jnp.dot(w_third, second, preferred_element_type=jnp.float32)  59.1 us
    dot_general x16, matrix products, regress(): jnp.dot(w_first, inputs, preferred_element_type=jnp.float32)  34 us
    ppermute x2, starting transfers between devices, with_halo(): lax.ppermute(lax.slice_in_dim(block, block.shape[dim] - width, None, axis...  6.67 us
    add x1, other arithmetic, shards(): return 0.75 * base_scores + 0.25 * (section_scores + dt_step * rate)  6.34 us
    transpose x1, local copies, waits for them, and re-layouts, sources(): return result.transpose(1, 0, 2).reshape(comps, count)  5.67 us
    ppermute x2, starting transfers between devices, with_halo(): lax.ppermute(lax.slice_in_dim(block, 0, width, axis=dim), axis, backward)  4.94 us
    unnamed x38, local copies, waits for them, and re-layouts  4.75 us
    another operation x1, local copies, waits for them, and re-layouts, shards(): sources(section_scores.reshape(comps, -1), weights)  4.73 us
  transfers between devices with their start and end apart: 6, of which 1 were waited for; matrix products, arithmetic and copies ran while one was open for 78% of the time, Pallas kernels for 0%

commit v1 on v0

--- a/solution.py
+++ b/solution.py
@@ -100,8 +100,9 @@
     owner = parcel_owner[:, 0]
     tiles_y = lax.axis_size("gy")
     capacity = max(2, 2 * blocks_here // tiles_y)
-    hits = (owner[:, None] == jnp.arange(tiles_y, dtype=jnp.int32)[None, :]).astype(jnp.int32)
-    ranks = jnp.sum(jnp.cumsum(hits, axis=0) * hits, axis=1) - 1
+    places = jnp.arange(blocks_here, dtype=jnp.int32)
+    earlier = (owner[None, :] == owner[:, None]) & (places[None, :] < places[:, None])
+    ranks = jnp.sum(earlier.astype(jnp.int32), axis=1)
     slot_ids = owner * capacity + ranks
     chosen = slot_ids[None, :] == jnp.arange(tiles_y * capacity, dtype=jnp.int32)[:, None]
     values = jnp.dot(chosen.astype(jnp.bfloat16), projected, preferred_element_type=jnp.float32)

time: 162 us -> 161 us (level)
  the two profiles are of different devices: /device:TPU:25 before, /device:TPU:17 now
where the time goes in v1:
time: 161 us; the launch traced here: 159 us
  matrix products  96.8 us (60%)
  local copies, waits for them, and re-layouts  31 us (19%)
  starting transfers between devices  19.5 us (12%)
  other arithmetic  8.97 us (6%)
  waiting for transfers between devices  2.72 us (2%)
    dot_general x16, matrix products, regress(): jnp.dot(w_third, second, preferred_element_type=jnp.float32)  59.1 us
    dot_general x16, matrix products, regress(): jnp.dot(w_first, inputs, preferred_element_type=jnp.float32)  34 us
    ppermute x2, starting transfers between devices, with_halo(): lax.ppermute(lax.slice_in_dim(block, block.shape[dim] - width, None, axis...  6.67 us
    add x1, other arithmetic, shards(): return 0.75 * base_scores + 0.25 * (section_scores + dt_step * rate)  6.58 us
    transpose x1, local copies, waits for them, and re-layouts, sources(): return result.transpose(1, 0, 2).reshape(comps, count)  5.67 us
    ppermute x2, starting transfers between devices, with_halo(): lax.ppermute(lax.slice_in_dim(block, 0, width, axis=dim), axis, backward)  4.94 us
    unnamed x42, local copies, waits for them, and re-layouts  4.75 us
    another operation x1, local copies, waits for them, and re-layouts, shards(): sources(section_scores.reshape(comps, -1), weights)  4.75 us
  transfers between devices with their start and end apart: 6, of which 1 were waited for; matrix products, arithmetic and copies ran while one was open for 78% of the time, Pallas kernels for 0%

profile of v1, /device:TPU:17, one launch (start us, length us, event | category | flops | bytes accessed | tf_op | source)
XLA Modules:
  0.0 159.5 jit_solution(11745315812802199296)
XLA Ops:
  0.0 0.9 convert_reduce_fusion
  0.9 0.7 multiply_add_fusion.2
  1.7 0.7 all_to_all.12
  2.4 3.8 %all-to-all-start = ((s32[4,16,1]{1,2,0:T(1,128)}), s32[4,16,1]{1,2,0:T(1,128)S(1)}, u32[]{:S(2)}, u32[]{:S(2)}) async-start(s32[4,16,1]{1,2,0:T(1,128)} %bitcast.9), calls=%async_computation | async-start | bytes 4096 | tf_op jit(solution)/shard_map/all_to_all | solution.py:112
  6.1 1.6 %fusion.28 = (f32[12,1,16,128]{3,2,1,0:T(8,128)}, f32[12,1,16,128]{3,2,1,0:T(8,128)}) fusion(f32[12,32,16,128]{3,2,1,0:T(8,128)} %param.17), kind=kLoop, calls=%fused_computation.50 | loop fusion | bytes 393216 | tf_op jit(solution)/shard_map/slice | solution.py:22
  7.8 3.1 %collective-permute-start.1 = (f32[12,1,16,128]{3,2,1,0:T(8,128)}, f32[12,1,16,128]{3,2,1,0:T(8,128)}, u32[]{:S(2)}, u32[]{:S(2)}) collective-permute-start(f32[12,1,16,128]{3,2,1,0:T(8,128)} %get-tuple-element.110), channel_id=1, source_target_pairs={{0,4},{4,8},{8,12},{12,16},{16,20},{20,24},{24,28},{1,5},{5,9},{9,... | collective-permute-start | bytes 294920 | tf_op jit(solution)/shard_map/ppermute | solution.py:19
  10.9 3.0 %collective-permute-start = (f32[12,1,16,128]{3,2,1,0:T(8,128)}, f32[12,1,16,128]{3,2,1,0:T(8,128)}, u32[]{:S(2)}, u32[]{:S(2)}) collective-permute-start(f32[12,1,16,128]{3,2,1,0:T(8,128)} %get-tuple-element.109), channel_id=1, source_target_pairs={{4,0},{8,4},{12,8},{16,12},{20,16},{24,20},{28,24},{5,1},{9,5},{13... | collective-permute-start | bytes 294920 | tf_op jit(solution)/shard_map/ppermute | solution.py:22
  14.1 3.0 %reshape_reshape.6 = bf16[12,16,4096]{2,1,0:T(8,128)(2,1)S(1)} reshape(f32[12,32,16,128]{3,2,1,0:T(8,128)} %param.17) | data formatting | bytes 4718592 | tf_op jit(solution)/shard_map/reshape;reshape | solution.py:41
  17.0 2.5 %fusion.13 = bf16[32,12,128]{2,1,0:T(8,128)(2,1)S(1)} fusion(bf16[32,300,128]{2,0,1:T(8,128)(2,1)} %param.27, bf16[12,300]{1,0:T(8,128)(2,1)S(1)} %copy-done), kind=kOutput, calls=%fused_computation.23 | convolution fusion | flops 29540352 | bytes 2563104 | tf_op jit(solution)/shard_map/ks,psc->pkc/dot_general | solution.py:96
  19.7 96.7 %while.10 = (s32[]{:T(128)}, f32[16,12,4096]{2,1,0:T(8,128)}, bf16[16,12,4096]{2,0,1:T(8,128)(2,1)S(1)}, bf16[256,12]{0,1:T(8,128)(2,1)S(1)}, f32[256]{0:T(256)S...) while((s32[]{:T(128)}, f32[16,12,4096]{2,1,0:T(8,128)}, ...), condition=%wide.region_1.2_spmd, body=%wide.region_0.1_spmd.sunk | while | flops 591446016 | bytes 4896933 | solution.py:42
  19.9 2.1 %fusion.46 = bf16[4096,256]{1,0:T(8,128)(2,1)} fusion(bf16[256,12]{0,1:T(8,128)(2,1)S(1)} %get-tuple-element.194, f32[256]{0:T(256)S(1)} %get-tuple-element.195, bf16[1,12,4096]{2,0,1:T(2,128)(2,1)S(1)} %constant_dynamic-slice_fusion.2), kind=kOutput, calls=%fused_computation.4.clone.1 | convolution fusion | flops 27262976 | bytes 2202624 | tf_op jit(solution)/shard_map/while/body/eval_jaxpr/dot_general | solution.py:30
  22.0 3.7 %fusion.47 = f32[16,12,4096]{2,1,0:T(8,128)} fusion(f32[16,12,4096]{2,1,0:T(8,128)} %get-tuple-element.182, s32[]{:T(128)S(6)} %copy.80, bf16[12,256]{1,0:T(8,128)(2,1)S(1)} %get-tuple-element.198, bf16[4096,256]{1,0:T(8,128)(2,1)} %fusion.46, bf16[256,256]{1,0:T(8,128)(2,1)S(1)} %get-tuple-element.196, f32[256]{0:T(256)S(1)} %get-tuple-element.197, ...), kind=kOutput, calls=%fused_computation.8.clone.1 | convolution fusion | flops 564183040 | bytes 2497588 | tf_op jit(solution)/shard_map/while/body/eval_jaxpr/dot_general | solution.py:35
  25.9 2.1 %fusion.46 = bf16[4096,256]{1,0:T(8,128)(2,1)} fusion(bf16[256,12]{0,1:T(8,128)(2,1)S(1)} %get-tuple-element.194, f32[256]{0:T(256)S(1)} %get-tuple-element.195, bf16[1,12,4096]{2,0,1:T(2,128)(2,1)S(1)} %constant_dynamic-slice_fusion.2), kind=kOutput, calls=%fused_computation.4.clone.1 | convolution fusion | flops 27262976 | bytes 2202624 | tf_op jit(solution)/shard_map/while/body/eval_jaxpr/dot_general | solution.py:30
  28.1 3.7 %fusion.47 = f32[16,12,4096]{2,1,0:T(8,128)} fusion(f32[16,12,4096]{2,1,0:T(8,128)} %get-tuple-element.182, s32[]{:T(128)S(6)} %copy.80, bf16[12,256]{1,0:T(8,128)(2,1)S(1)} %get-tuple-element.198, bf16[4096,256]{1,0:T(8,128)(2,1)} %fusion.46, bf16[256,256]{1,0:T(8,128)(2,1)S(1)} %get-tuple-element.196, f32[256]{0:T(256)S(1)} %get-tuple-element.197, ...), kind=kOutput, calls=%fused_computation.8.clone.1 | convolution fusion | flops 564183040 | bytes 2497588 | tf_op jit(solution)/shard_map/while/body/eval_jaxpr/dot_general | solution.py:35
  32.0 2.1 %fusion.46 = bf16[4096,256]{1,0:T(8,128)(2,1)} fusion(bf16[256,12]{0,1:T(8,128)(2,1)S(1)} %get-tuple-element.194, f32[256]{0:T(256)S(1)} %get-tuple-element.195, bf16[1,12,4096]{2,0,1:T(2,128)(2,1)S(1)} %constant_dynamic-slice_fusion.2), kind=kOutput, calls=%fused_computation.4.clone.1 | convolution fusion | flops 27262976 | bytes 2202624 | tf_op jit(solution)/shard_map/while/body/eval_jaxpr/dot_general | solution.py:30
  34.1 3.7 %fusion.47 = f32[16,12,4096]{2,1,0:T(8,128)} fusion(f32[16,12,4096]{2,1,0:T(8,128)} %get-tuple-element.182, s32[]{:T(128)S(6)} %copy.80, bf16[12,256]{1,0:T(8,128)(2,1)S(1)} %get-tuple-element.198, bf16[4096,256]{1,0:T(8,128)(2,1)} %fusion.46, bf16[256,256]{1,0:T(8,128)(2,1)S(1)} %get-tuple-element.196, f32[256]{0:T(256)S(1)} %get-tuple-element.197, ...), kind=kOutput, calls=%fused_computation.8.clone.1 | convolution fusion | flops 564183040 | bytes 2497588 | tf_op jit(solution)/shard_map/while/body/eval_jaxpr/dot_general | solution.py:35
  38.0 2.1 %fusion.46 = bf16[4096,256]{1,0:T(8,128)(2,1)} fusion(bf16[256,12]{0,1:T(8,128)(2,1)S(1)} %get-tuple-element.194, f32[256]{0:T(256)S(1)} %get-tuple-element.195, bf16[1,12,4096]{2,0,1:T(2,128)(2,1)S(1)} %constant_dynamic-slice_fusion.2), kind=kOutput, calls=%fused_computation.4.clone.1 | convolution fusion | flops 27262976 | bytes 2202624 | tf_op jit(solution)/shard_map/while/body/eval_jaxpr/dot_general | solution.py:30
  40.1 3.7 %fusion.47 = f32[16,12,4096]{2,1,0:T(8,128)} fusion(f32[16,12,4096]{2,1,0:T(8,128)} %get-tuple-element.182, s32[]{:T(128)S(6)} %copy.80, bf16[12,256]{1,0:T(8,128)(2,1)S(1)} %get-tuple-element.198, bf16[4096,256]{1,0:T(8,128)(2,1)} %fusion.46, bf16[256,256]{1,0:T(8,128)(2,1)S(1)} %get-tuple-element.196, f32[256]{0:T(256)S(1)} %get-tuple-element.197, ...), kind=kOutput, calls=%fused_computation.8.clone.1 | convolution fusion | flops 564183040 | bytes 2497588 | tf_op jit(solution)/shard_map/while/body/eval_jaxpr/dot_general | solution.py:35
  44.1 2.1 %fusion.46 = bf16[4096,256]{1,0:T(8,128)(2,1)} fusion(bf16[256,12]{0,1:T(8,128)(2,1)S(1)} %get-tuple-element.194, f32[256]{0:T(256)S(1)} %get-tuple-element.195, bf16[1,12,4096]{2,0,1:T(2,128)(2,1)S(1)} %constant_dynamic-slice_fusion.2), kind=kOutput, calls=%fused_computation.4.clone.1 | convolution fusion | flops 27262976 | bytes 2202624 | tf_op jit(solution)/shard_map/while/body/eval_jaxpr/dot_general | solution.py:30
  46.2 3.7 %fusion.47 = f32[16,12,4096]{2,1,0:T(8,128)} fusion(f32[16,12,4096]{2,1,0:T(8,128)} %get-tuple-element.182, s32[]{:T(128)S(6)} %copy.80, bf16[12,256]{1,0:T(8,128)(2,1)S(1)} %get-tuple-element.198, bf16[4096,256]{1,0:T(8,128)(2,1)} %fusion.46, bf16[256,256]{1,0:T(8,128)(2,1)S(1)} %get-tuple-element.196, f32[256]{0:T(256)S(1)} %get-tuple-element.197, ...), kind=kOutput, calls=%fused_computation.8.clone.1 | convolution fusion | flops 564183040 | bytes 2497588 | tf_op jit(solution)/shard_map/while/body/eval_jaxpr/dot_general | solution.py:35
  50.1 2.1 %fusion.46 = bf16[4096,256]{1,0:T(8,128)(2,1)} fusion(bf16[256,12]{0,1:T(8,128)(2,1)S(1)} %get-tuple-element.194, f32[256]{0:T(256)S(1)} %get-tuple-element.195, bf16[1,12,4096]{2,0,1:T(2,128)(2,1)S(1)} %constant_dynamic-slice_fusion.2), kind=kOutput, calls=%fused_computation.4.clone.1 | convolution fusion | flops 27262976 | bytes 2202624 | tf_op jit(solution)/shard_map/while/body/eval_jaxpr/dot_general | solution.py:30
  52.2 3.7 %fusion.47 = f32[16,12,4096]{2,1,0:T(8,128)} fusion(f32[16,12,4096]{2,1,0:T(8,128)} %get-tuple-element.182, s32[]{:T(128)S(6)} %copy.80, bf16[12,256]{1,0:T(8,128)(2,1)S(1)} %get-tuple-element.198, bf16[4096,256]{1,0:T(8,128)(2,1)} %fusion.46, bf16[256,256]{1,0:T(8,128)(2,1)S(1)} %get-tuple-element.196, f32[256]{0:T(256)S(1)} %get-tuple-element.197, ...), kind=kOutput, calls=%fused_computation.8.clone.1 | convolution fusion | flops 564183040 | bytes 2497588 | tf_op jit(solution)/shard_map/while/body/eval_jaxpr/dot_general | solution.py:35
  56.1 2.1 %fusion.46 = bf16[4096,256]{1,0:T(8,128)(2,1)} fusion(bf16[256,12]{0,1:T(8,128)(2,1)S(1)} %get-tuple-element.194, f32[256]{0:T(256)S(1)} %get-tuple-element.195, bf16[1,12,4096]{2,0,1:T(2,128)(2,1)S(1)} %constant_dynamic-slice_fusion.2), kind=kOutput, calls=%fused_computation.4.clone.1 | convolution fusion | flops 27262976 | bytes 2202624 | tf_op jit(solution)/shard_map/while/body/eval_jaxpr/dot_general | solution.py:30
  58.3 3.7 %fusion.47 = f32[16,12,4096]{2,1,0:T(8,128)} fusion(f32[16,12,4096]{2,1,0:T(8,128)} %get-tuple-element.182, s32[]{:T(128)S(6)} %copy.80, bf16[12,256]{1,0:T(8,128)(2,1)S(1)} %get-tuple-element.198, bf16[4096,256]{1,0:T(8,128)(2,1)} %fusion.46, bf16[256,256]{1,0:T(8,128)(2,1)S(1)} %get-tuple-element.196, f32[256]{0:T(256)S(1)} %get-tuple-element.197, ...), kind=kOutput, calls=%fused_computation.8.clone.1 | convolution fusion | flops 564183040 | bytes 2497588 | tf_op jit(solution)/shard_map/while/body/eval_jaxpr/dot_general | solution.py:35
  62.2 2.1 %fusion.46 = bf16[4096,256]{1,0:T(8,128)(2,1)} fusion(bf16[256,12]{0,1:T(8,128)(2,1)S(1)} %get-tuple-element.194, f32[256]{0:T(256)S(1)} %get-tuple-element.195, bf16[1,12,4096]{2,0,1:T(2,128)(2,1)S(1)} %constant_dynamic-slice_fusion.2), kind=kOutput, calls=%fused_computation.4.clone.1 | convolution fusion | flops 27262976 | bytes 2202624 | tf_op jit(solution)/shard_map/while/body/eval_jaxpr/dot_general | solution.py:30
  64.3 3.7 %fusion.47 = f32[16,12,4096]{2,1,0:T(8,128)} fusion(f32[16,12,4096]{2,1,0:T(8,128)} %get-tuple-element.182, s32[]{:T(128)S(6)} %copy.80, bf16[12,256]{1,0:T(8,128)(2,1)S(1)} %get-tuple-element.198, bf16[4096,256]{1,0:T(8,128)(2,1)} %fusion.46, bf16[256,256]{1,0:T(8,128)(2,1)S(1)} %get-tuple-element.196, f32[256]{0:T(256)S(1)} %get-tuple-element.197, ...), kind=kOutput, calls=%fused_computation.8.clone.1 | convolution fusion | flops 564183040 | bytes 2497588 | tf_op jit(solution)/shard_map/while/body/eval_jaxpr/dot_general | solution.py:35
  68.2 2.1 %fusion.46 = bf16[4096,256]{1,0:T(8,128)(2,1)} fusion(bf16[256,12]{0,1:T(8,128)(2,1)S(1)} %get-tuple-element.194, f32[256]{0:T(256)S(1)} %get-tuple-element.195, bf16[1,12,4096]{2,0,1:T(2,128)(2,1)S(1)} %constant_dynamic-slice_fusion.2), kind=kOutput, calls=%fused_computation.4.clone.1 | convolution fusion | flops 27262976 | bytes 2202624 | tf_op jit(solution)/shard_map/while/body/eval_jaxpr/dot_general | solution.py:30
  70.4 3.7 %fusion.47 = f32[16,12,4096]{2,1,0:T(8,128)} fusion(f32[16,12,4096]{2,1,0:T(8,128)} %get-tuple-element.182, s32[]{:T(128)S(6)} %copy.80, bf16[12,256]{1,0:T(8,128)(2,1)S(1)} %get-tuple-element.198, bf16[4096,256]{1,0:T(8,128)(2,1)} %fusion.46, bf16[256,256]{1,0:T(8,128)(2,1)S(1)} %get-tuple-element.196, f32[256]{0:T(256)S(1)} %get-tuple-element.197, ...), kind=kOutput, calls=%fused_computation.8.clone.1 | convolution fusion | flops 564183040 | bytes 2497588 | tf_op jit(solution)/shard_map/while/body/eval_jaxpr/dot_general | solution.py:35
  74.3 2.1 %fusion.46 = bf16[4096,256]{1,0:T(8,128)(2,1)} fusion(bf16[256,12]{0,1:T(8,128)(2,1)S(1)} %get-tuple-element.194, f32[256]{0:T(256)S(1)} %get-tuple-element.195, bf16[1,12,4096]{2,0,1:T(2,128)(2,1)S(1)} %constant_dynamic-slice_fusion.2), kind=kOutput, calls=%fused_computation.4.clone.1 | convolution fusion | flops 27262976 | bytes 2202624 | tf_op jit(solution)/shard_map/while/body/eval_jaxpr/dot_general | solution.py:30
  76.4 3.7 %fusion.47 = f32[16,12,4096]{2,1,0:T(8,128)} fusion(f32[16,12,4096]{2,1,0:T(8,128)} %get-tuple-element.182, s32[]{:T(128)S(6)} %copy.80, bf16[12,256]{1,0:T(8,128)(2,1)S(1)} %get-tuple-element.198, bf16[4096,256]{1,0:T(8,128)(2,1)} %fusion.46, bf16[256,256]{1,0:T(8,128)(2,1)S(1)} %get-tuple-element.196, f32[256]{0:T(256)S(1)} %get-tuple-element.197, ...), kind=kOutput, calls=%fused_computation.8.clone.1 | convolution fusion | flops 564183040 | bytes 2497588 | tf_op jit(solution)/shard_map/while/body/eval_jaxpr/dot_general | solution.py:35
  80.3 2.1 %fusion.46 = bf16[4096,256]{1,0:T(8,128)(2,1)} fusion(bf16[256,12]{0,1:T(8,128)(2,1)S(1)} %get-tuple-element.194, f32[256]{0:T(256)S(1)} %get-tuple-element.195, bf16[1,12,4096]{2,0,1:T(2,128)(2,1)S(1)} %constant_dynamic-slice_fusion.2), kind=kOutput, calls=%fused_computation.4.clone.1 | convolution fusion | flops 27262976 | bytes 2202624 | tf_op jit(solution)/shard_map/while/body/eval_jaxpr/dot_general | solution.py:30
  82.4 3.7 %fusion.47 = f32[16,12,4096]{2,1,0:T(8,128)} fusion(f32[16,12,4096]{2,1,0:T(8,128)} %get-tuple-element.182, s32[]{:T(128)S(6)} %copy.80, bf16[12,256]{1,0:T(8,128)(2,1)S(1)} %get-tuple-element.198, bf16[4096,256]{1,0:T(8,128)(2,1)} %fusion.46, bf16[256,256]{1,0:T(8,128)(2,1)S(1)} %get-tuple-element.196, f32[256]{0:T(256)S(1)} %get-tuple-element.197, ...), kind=kOutput, calls=%fused_computation.8.clone.1 | convolution fusion | flops 564183040 | bytes 2497588 | tf_op jit(solution)/shard_map/while/body/eval_jaxpr/dot_general | solution.py:35
  86.4 2.1 %fusion.46 = bf16[4096,256]{1,0:T(8,128)(2,1)} fusion(bf16[256,12]{0,1:T(8,128)(2,1)S(1)} %get-tuple-element.194, f32[256]{0:T(256)S(1)} %get-tuple-element.195, bf16[1,12,4096]{2,0,1:T(2,128)(2,1)S(1)} %constant_dynamic-slice_fusion.2), kind=kOutput, calls=%fused_computation.4.clone.1 | convolution fusion | flops 27262976 | bytes 2202624 | tf_op jit(solution)/shard_map/while/body/eval_jaxpr/dot_general | solution.py:30
  88.5 3.7 %fusion.47 = f32[16,12,4096]{2,1,0:T(8,128)} fusion(f32[16,12,4096]{2,1,0:T(8,128)} %get-tuple-element.182, s32[]{:T(128)S(6)} %copy.80, bf16[12,256]{1,0:T(8,128)(2,1)S(1)} %get-tuple-element.198, bf16[4096,256]{1,0:T(8,128)(2,1)} %fusion.46, bf16[256,256]{1,0:T(8,128)(2,1)S(1)} %get-tuple-element.196, f32[256]{0:T(256)S(1)} %get-tuple-element.197, ...), kind=kOutput, calls=%fused_computation.8.clone.1 | convolution fusion | flops 564183040 | bytes 2497588 | tf_op jit(solution)/shard_map/while/body/eval_jaxpr/dot_general | solution.py:35
  92.4 2.1 %fusion.46 = bf16[4096,256]{1,0:T(8,128)(2,1)} fusion(bf16[256,12]{0,1:T(8,128)(2,1)S(1)} %get-tuple-element.194, f32[256]{0:T(256)S(1)} %get-tuple-element.195, bf16[1,12,4096]{2,0,1:T(2,128)(2,1)S(1)} %constant_dynamic-slice_fusion.2), kind=kOutput, calls=%fused_computation.4.clone.1 | convolution fusion | flops 27262976 | bytes 2202624 | tf_op jit(solution)/shard_map/while/body/eval_jaxpr/dot_general | solution.py:30
  94.6 3.7 %fusion.47 = f32[16,12,4096]{2,1,0:T(8,128)} fusion(f32[16,12,4096]{2,1,0:T(8,128)} %get-tuple-element.182, s32[]{:T(128)S(6)} %copy.80, bf16[12,256]{1,0:T(8,128)(2,1)S(1)} %get-tuple-element.198, bf16[4096,256]{1,0:T(8,128)(2,1)} %fusion.46, bf16[256,256]{1,0:T(8,128)(2,1)S(1)} %get-tuple-element.196, f32[256]{0:T(256)S(1)} %get-tuple-element.197, ...), kind=kOutput, calls=%fused_computation.8.clone.1 | convolution fusion | flops 564183040 | bytes 2497588 | tf_op jit(solution)/shard_map/while/body/eval_jaxpr/dot_general | solution.py:35
  98.5 2.1 %fusion.46 = bf16[4096,256]{1,0:T(8,128)(2,1)} fusion(bf16[256,12]{0,1:T(8,128)(2,1)S(1)} %get-tuple-element.194, f32[256]{0:T(256)S(1)} %get-tuple-element.195, bf16[1,12,4096]{2,0,1:T(2,128)(2,1)S(1)} %constant_dynamic-slice_fusion.2), kind=kOutput, calls=%fused_computation.4.clone.1 | convolution fusion | flops 27262976 | bytes 2202624 | tf_op jit(solution)/shard_map/while/body/eval_jaxpr/dot_general | solution.py:30
  100.6 3.7 %fusion.47 = f32[16,12,4096]{2,1,0:T(8,128)} fusion(f32[16,12,4096]{2,1,0:T(8,128)} %get-tuple-element.182, s32[]{:T(128)S(6)} %copy.80, bf16[12,256]{1,0:T(8,128)(2,1)S(1)} %get-tuple-element.198, bf16[4096,256]{1,0:T(8,128)(2,1)} %fusion.46, bf16[256,256]{1,0:T(8,128)(2,1)S(1)} %get-tuple-element.196, f32[256]{0:T(256)S(1)} %get-tuple-element.197, ...), kind=kOutput, calls=%fused_computation.8.clone.1 | convolution fusion | flops 564183040 | bytes 2497588 | tf_op jit(solution)/shard_map/while/body/eval_jaxpr/dot_general | solution.py:35
  104.5 2.1 %fusion.46 = bf16[4096,256]{1,0:T(8,128)(2,1)} fusion(bf16[256,12]{0,1:T(8,128)(2,1)S(1)} %get-tuple-element.194, f32[256]{0:T(256)S(1)} %get-tuple-element.195, bf16[1,12,4096]{2,0,1:T(2,128)(2,1)S(1)} %constant_dynamic-slice_fusion.2), kind=kOutput, calls=%fused_computation.4.clone.1 | convolution fusion | flops 27262976 | bytes 2202624 | tf_op jit(solution)/shard_map/while/body/eval_jaxpr/dot_general | solution.py:30
  106.6 3.7 %fusion.47 = f32[16,12,4096]{2,1,0:T(8,128)} fusion(f32[16,12,4096]{2,1,0:T(8,128)} %get-tuple-element.182, s32[]{:T(128)S(6)} %copy.80, bf16[12,256]{1,0:T(8,128)(2,1)S(1)} %get-tuple-element.198, bf16[4096,256]{1,0:T(8,128)(2,1)} %fusion.46, bf16[256,256]{1,0:T(8,128)(2,1)S(1)} %get-tuple-element.196, f32[256]{0:T(256)S(1)} %get-tuple-element.197, ...), kind=kOutput, calls=%fused_computation.8.clone.1 | convolution fusion | flops 564183040 | bytes 2497588 | tf_op jit(solution)/shard_map/while/body/eval_jaxpr/dot_general | solution.py:35
  110.5 2.1 %fusion.46 = bf16[4096,256]{1,0:T(8,128)(2,1)} fusion(bf16[256,12]{0,1:T(8,128)(2,1)S(1)} %get-tuple-element.194, f32[256]{0:T(256)S(1)} %get-tuple-element.195, bf16[1,12,4096]{2,0,1:T(2,128)(2,1)S(1)} %constant_dynamic-slice_fusion.2), kind=kOutput, calls=%fused_computation.4.clone.1 | convolution fusion | flops 27262976 | bytes 2202624 | tf_op jit(solution)/shard_map/while/body/eval_jaxpr/dot_general | solution.py:30
  112.7 3.7 %fusion.47 = f32[16,12,4096]{2,1,0:T(8,128)} fusion(f32[16,12,4096]{2,1,0:T(8,128)} %get-tuple-element.182, s32[]{:T(128)S(6)} %copy.80, bf16[12,256]{1,0:T(8,128)(2,1)S(1)} %get-tuple-element.198, bf16[4096,256]{1,0:T(8,128)(2,1)} %fusion.46, bf16[256,256]{1,0:T(8,128)(2,1)S(1)} %get-tuple-element.196, f32[256]{0:T(256)S(1)} %get-tuple-element.197, ...), kind=kOutput, calls=%fused_computation.8.clone.1 | convolution fusion | flops 564183040 | bytes 2497588 | tf_op jit(solution)/shard_map/while/body/eval_jaxpr/dot_general | solution.py:35
  116.4 0.9 slice_bitcast_fusion.2
  117.3 1.0 fusion.18
  118.3 5.7 %copy.53 = f32[12,16,4096]{2,1,0:T(8,128)} copy(f32[12,16,4096]{2,0,1:T(8,128)} %bitcast.66) | data formatting | bytes 6291456 | tf_op jit(solution)/shard_map/transpose | solution.py:43
  124.0 4.7 %reshape_reshape.7 = f32[12,32,16,128]{3,2,1,0:T(8,128)} reshape(f32[12,16,4096]{2,1,0:T(8,128)} %copy.53) | data formatting | bytes 6291456 | tf_op jit(solution)/shard_map/reshape;reshape | solution.py:93
  128.8 0.6 copy-done.10
  129.3 4.1 %all-to-all-start.1 = ((f32[4,16,1536]{2,1,0:T(8,128)}), f32[4,16,1536]{2,1,0:T(8,128)S(1)}, u32[]{:S(2)}, u32[]{:S(2)}) async-start(f32[4,16,1536]{2,1,0:T(8,128)} %fusion.18), calls=%async_computation.1 | async-start | bytes 786432 | tf_op jit(solution)/shard_map/all_to_all | solution.py:111
  133.4 0.7 add_reduce_fusion
  134.1 0.6 sub.27
  134.7 0.9 constant_dynamic-update-slice_fusion.2
  135.6 0.3 constant_dynamic-update-slice_fusion.1
  135.9 0.9 constant_dynamic-update-slice_fusion
  136.8 1.7 %copy-done.3 = f32[12,34,16,128]{3,2,1,0:T(8,128)} copy-done((f32[12,34,16,128]{3,2,1,0:T(8,128)}, f32[12,34,16,128]{3,2,1,0:T(8,128)S(1)}, u32[]{:S(2)}) %copy-start.3) | copy-done | bytes 3342360
  138.5 0.3 fusion.27
  138.8 0.7 copy.50
  139.5 3.5 %collective-permute-start.3 = (f32[12,34,1,128]{3,1,2,0:T(8,128)}, f32[12,34,1,128]{3,1,2,0:T(8,128)}, u32[]{:S(2)}, u32[]{:S(2)}) collective-permute-start(f32[12,34,1,128]{3,1,2,0:T(8,128)} %copy.50), channel_id=1, source_target_pairs={{0,1},{1,2},{2,3},{4,5},{5,6},{6,7},{8,9},{9,10},{10,11},{12,13},{... | collective-permute-start | bytes 626696 | tf_op jit(solution)/shard_map/ppermute | solution.py:19
  143.1 0.8 copy.48
  143.8 1.9 %collective-permute-start.2 = (f32[12,34,1,128]{3,1,2,0:T(8,128)}, f32[12,34,1,128]{3,1,2,0:T(8,128)}, u32[]{:S(2)}, u32[]{:S(2)}) collective-permute-start(f32[12,34,1,128]{3,1,2,0:T(8,128)} %copy.48), channel_id=1, source_target_pairs={{1,0},{2,1},{3,2},{5,4},{6,5},{7,6},{9,8},{10,9},{11,10},{13,12},{... | collective-permute-start | bytes 626696 | tf_op jit(solution)/shard_map/ppermute | solution.py:22
  146.5 0.8 copy.60
  147.6 1.3 copy.51
  149.0 2.7 %collective-permute-done.2 = f32[12,34,1,128]{3,1,2,0:T(8,128)} collective-permute-done((f32[12,34,1,128]{3,1,2,0:T(8,128)}, f32[12,34,1,128]{3,1,2,0:T(8,128)}, u32[]{:S(2)}, u32[]{:S(2)}) %collective-permute-start.2) | collective-permute-done | bytes 208928 | tf_op jit(solution)/shard_map/ppermute | solution.py:22
  151.7 1.2 copy.49
  152.9 6.6 %multiply_add_fusion = f32[12,32,16,128]{3,2,1,0:T(8,128)} fusion(f32[12,32,16,128]{3,2,1,0:T(8,128)S(1)} %copy-done.1, f32[12,32,16,128]{3,2,1,0:T(8,128)S(1)} %bitcast.65, f32[12,32,16,128]{3,2,1,0:T(8,128)S(1)} %copy-done.2, f32[12,34,16,128]{3,2,1,0:T(8,128)S(1)} %copy-done.4, f32[12,34,1,128]{3,2,1,0:T(1,128)S(1)} %copy.51, ...), kind=kLoop, calls=%fused_computation.18 | loop fusion | flops 22806528 | bytes 20733952 | tf_op jit(solution)/shard_map/add | solution.py:124
  (64 shorter events, 4.7 us)
Async XLA Ops:
  0.0 17.0 %copy-start = (bf16[12,300]{1,0:T(8,128)(2,1)S(1)}, bf16[12,300]{1,0:T(8,128)(2,1)}, u32[]{:S(2)}) copy-start(bf16[12,300]{1,0:T(8,128)(2,1)} %param.26) | copy-start | bytes 21604
  2.4 126.4 %all-to-all-start = ((s32[4,16,1]{1,2,0:T(1,128)}), s32[4,16,1]{1,2,0:T(1,128)S(1)}, u32[]{:S(2)}, u32[]{:S(2)}) async-start(s32[4,16,1]{1,2,0:T(1,128)} %bitcast.9), calls=%async_computation | async-start | bytes 4096 | tf_op jit(solution)/shard_map/all_to_all | solution.py:112
  7.8 126.9 %collective-permute-start.1 = (f32[12,1,16,128]{3,2,1,0:T(8,128)}, f32[12,1,16,128]{3,2,1,0:T(8,128)}, u32[]{:S(2)}, u32[]{:S(2)}) collective-permute-start(f32[12,1,16,128]{3,2,1,0:T(8,128)} %get-tuple-element.110), channel_id=1, source_target_pairs={{0,4},{4,8},{8,12},{12,16},{16,20},{20,24},{24,28},{1,5},{5,9},{9,... | collective-permute-start | bytes 294920 | tf_op jit(solution)/shard_map/ppermute | solution.py:19
  10.9 125.0 %collective-permute-start = (f32[12,1,16,128]{3,2,1,0:T(8,128)}, f32[12,1,16,128]{3,2,1,0:T(8,128)}, u32[]{:S(2)}, u32[]{:S(2)}) collective-permute-start(f32[12,1,16,128]{3,2,1,0:T(8,128)} %get-tuple-element.109), channel_id=1, source_target_pairs={{4,0},{8,4},{12,8},{16,12},{20,16},{24,20},{28,24},{5,1},{9,5},{13... | collective-permute-start | bytes 294920 | tf_op jit(solution)/shard_map/ppermute | solution.py:22
  14.0 5.6 %copy-start.12 = (bf16[256,256]{1,0:T(8,128)(2,1)S(1)}, bf16[256,256]{1,0:T(8,128)(2,1)}, u32[]{:S(2)}) copy-start(bf16[256,256]{1,0:T(8,128)(2,1)} %param.22) | copy-start | bytes 393220
  14.0 5.6 %copy-start.13 = (bf16[256,12]{0,1:T(8,128)(2,1)S(1)}, bf16[256,12]{0,1:T(8,128)(2,1)}, u32[]{:S(2)}) copy-start(bf16[256,12]{0,1:T(8,128)(2,1)} %param.20) | copy-start | bytes 18436
  14.0 5.6 %copy-start.14 = (bf16[12,256]{1,0:T(8,128)(2,1)S(1)}, bf16[12,256]{1,0:T(8,128)(2,1)}, u32[]{:S(2)}) copy-start(bf16[12,256]{1,0:T(8,128)(2,1)} %param.24) | copy-start | bytes 18436
  14.0 5.6 %copy-start.15 = (f32[256]{0:T(256)S(1)}, f32[256]{0:T(256)}, u32[]{:S(2)}) copy-start(f32[256]{0:T(256)} %param.21) | copy-start | bytes 3076
  14.0 5.6 %copy-start.16 = (f32[256]{0:T(256)S(1)}, f32[256]{0:T(256)}, u32[]{:S(2)}) copy-start(f32[256]{0:T(256)} %param.23) | copy-start | bytes 3076
  14.0 5.6 %copy-start.17 = (f32[12]{0:T(128)S(1)}, f32[12]{0:T(128)}, u32[]{:S(2)}) copy-start(f32[12]{0:T(128)} %param.25) | copy-start | bytes 148
  19.6 96.7 %copy-start.8 = (f32[3,32,16,128]{3,2,1,0:T(8,128)S(1)}, f32[3,32,16,128]{3,2,1,0:T(8,128)}, u32[]{:S(2)}) copy-start(f32[3,32,16,128]{3,2,1,0:T(8,128)} %param.18) | copy-start | bytes 2359300
  124.0 11.6 %copy-start.1 = (f32[12,32,16,128]{3,2,1,0:T(8,128)S(1)}, f32[12,32,16,128]{3,2,1,0:T(8,128)}, u32[]{:S(2)}) copy-start(f32[12,32,16,128]{3,2,1,0:T(8,128)} %param.17) | copy-start | bytes 9437188
  128.8 0.6 copy-start.10
  129.3 16.4 %all-to-all-start.1 = ((f32[4,16,1536]{2,1,0:T(8,128)}), f32[4,16,1536]{2,1,0:T(8,128)S(1)}, u32[]{:S(2)}, u32[]{:S(2)}) async-start(f32[4,16,1536]{2,1,0:T(8,128)} %fusion.18), calls=%async_computation.1 | async-start | bytes 786432 | tf_op jit(solution)/shard_map/all_to_all | solution.py:111
  135.6 10.2 %copy-start.11 = (s32[64]{0:T(128)S(1)}, s32[64]{0:T(128)}, u32[]{:S(2)}) copy-start(s32[64]{0:T(128)} %sub.27) | copy-start | bytes 772
  136.8 1.7 %copy-start.3 = (f32[12,34,16,128]{3,2,1,0:T(8,128)}, f32[12,34,16,128]{3,2,1,0:T(8,128)S(1)}, u32[]{:S(2)}) copy-start(f32[12,34,16,128]{3,2,1,0:T(8,128)S(1)} %constant_dynamic-update-slice_fusion) | copy-start | bytes 10027012
  139.5 8.1 %collective-permute-start.3 = (f32[12,34,1,128]{3,1,2,0:T(8,128)}, f32[12,34,1,128]{3,1,2,0:T(8,128)}, u32[]{:S(2)}, u32[]{:S(2)}) collective-permute-start(f32[12,34,1,128]{3,1,2,0:T(8,128)} %copy.50), channel_id=1, source_target_pairs={{0,1},{1,2},{2,3},{4,5},{5,6},{6,7},{8,9},{9,10},{10,11},{12,13},{... | collective-permute-start | bytes 626696 | tf_op jit(solution)/shard_map/ppermute | solution.py:19
  143.8 7.8 %collective-permute-start.2 = (f32[12,34,1,128]{3,1,2,0:T(8,128)}, f32[12,34,1,128]{3,1,2,0:T(8,128)}, u32[]{:S(2)}, u32[]{:S(2)}) collective-permute-start(f32[12,34,1,128]{3,1,2,0:T(8,128)} %copy.48), channel_id=1, source_target_pairs={{1,0},{2,1},{3,2},{5,4},{6,5},{7,6},{9,8},{10,9},{11,10},{13,12},{... | collective-permute-start | bytes 626696 | tf_op jit(solution)/shard_map/ppermute | solution.py:22
  146.5 6.3 %copy-start.7 = (f32[32,16,128]{2,1,0:T(8,128)S(1)}, f32[32,16,128]{2,1,0:T(8,128)}, u32[]{:S(2)}) copy-start(f32[32,16,128]{2,1,0:T(8,128)} %get-tuple-element.113) | copy-start | bytes 786436
  146.5 6.3 %copy-start.9 = (f32[32,16,128]{2,1,0:T(8,128)S(1)}, f32[32,16,128]{2,1,0:T(8,128)}, u32[]{:S(2)}) copy-start(f32[32,16,128]{2,1,0:T(8,128)} %param.19) | copy-start | bytes 786436
  147.4 5.5 %copy-start.2 = (f32[12,32,16,128]{3,2,1,0:T(8,128)S(1)}, f32[12,32,16,128]{3,2,1,0:T(8,128)}, u32[]{:S(2)}) copy-start(f32[12,32,16,128]{3,2,1,0:T(8,128)} %reshape_reshape.7) | copy-start | bytes 9437188
  147.4 5.5 %copy-start.4 = (f32[12,34,16,128]{3,2,1,0:T(8,128)S(1)}, f32[12,34,16,128]{3,2,1,0:T(8,128)}, u32[]{:S(2)}) copy-start(f32[12,34,16,128]{3,2,1,0:T(8,128)} %copy-done.3) | copy-start | bytes 10027012
  147.4 5.5 %copy-start.5 = (f32[32,16,128]{2,1,0:T(8,128)S(1)}, f32[32,16,128]{2,1,0:T(8,128)}, u32[]{:S(2)}) copy-start(f32[32,16,128]{2,1,0:T(8,128)} %get-tuple-element.111) | copy-start | bytes 786436
  147.4 5.5 %copy-start.6 = (f32[32,16,128]{2,1,0:T(8,128)S(1)}, f32[32,16,128]{2,1,0:T(8,128)}, u32[]{:S(2)}) copy-start(f32[32,16,128]{2,1,0:T(8,128)} %get-tuple-element.112) | copy-start | bytes 786436

commit v2 on v0

v2 whole, which is shorter than its diff:
```python
import functools

import jax
import jax.numpy as jnp
from jax import lax
from jax.experimental import pallas as pl
from jax.experimental.pallas import tpu as pltpu
from jax.sharding import PartitionSpec as P

SB = 32

dt_step = 0.25
keep_base = 0.75
keep_section = 0.25
scale = keep_section * dt_step

TILE = 256
f32, bf16 = jnp.float32, jnp.bfloat16


def bias_column(row, width):
    return jnp.transpose(jnp.broadcast_to(row, (width, row.shape[1])))


def prepare_weights(w1t, b1, w2, b2, w3, b3, w1_s, b2_s, w3_s, b3_s):
    comps, hidden = w1t.shape
    bias = b1[...]
    high = bias.astype(bf16).astype(f32)
    middle = (bias - high).astype(bf16).astype(f32)
    low = (bias - high - middle).astype(bf16).astype(f32)
    rows = jnp.concatenate(
        [w1t[...].astype(f32), high, middle, low]
        + [jnp.zeros((128 - comps - 3, hidden), f32)],
        axis=0,
    )
    first = jnp.transpose(rows).astype(bf16)
    w1_s[...] = jnp.concatenate(
        [first, jnp.zeros((hidden, TILE - 128), bf16)], axis=1
    )
    b2_s[...] = bias_column(b2[...], 128)
    w3_s[...] = jnp.concatenate(
        [w3[...].astype(f32), jnp.zeros((16 - comps, hidden), f32)], axis=0
    ).astype(bf16)
    row = jnp.concatenate([b3[...], jnp.zeros((1, 128 - comps), f32)], axis=1)
    b3_s[...] = bias_column(row, 128)[:16]


def regression_stages(
    cells, comps, planes, rows_y, w1_s, w2, b2_s, w3_s, b3_s, first_s, second_s, accs, put
):
    total = cells.shape[0] // comps
    across = TILE // 128
    tiles = rows_y // across
    ones = jnp.ones((16 - comps, 128), f32)
    empty = jnp.zeros((TILE - 16, TILE), bf16)
    first_acc, second_acc, third_acc = accs

    def widen(column):
        return jnp.concatenate([column] * across, axis=1)

    def layer1(row0, slot, tile):
        mxu = tile % 2
        parts = []
        for k in range(across):
            part = cells[pl.ds(row0 + tile * across + k, comps, stride=total), :]
            parts.append(jnp.concatenate([part, ones], axis=0).astype(bf16))
        block = jnp.concatenate([jnp.concatenate(parts, axis=1), empty], axis=0)
        pltpu.matmul_push_rhs(block, 0, mxu)
        pltpu.matmul_acc_lhs(first_acc[mxu], w1_s[...], load_staged_rhs=0)

        def finish():
            out = pltpu.matmul_pop(first_acc[mxu])
            first_s[slot][:, pl.ds(tile * TILE, TILE)] = jnp.tanh(out).astype(bf16)

        return finish

    def layer2(slot, tile):
        mxu = tile % 2
        pltpu.matmul_push_rhs(first_s[slot][:, pl.ds(tile * TILE, TILE)], 1, mxu)
        pltpu.matmul_acc_lhs(second_acc[mxu], w2[...], load_staged_rhs=1)

        def finish():
            out = pltpu.matmul_pop(second_acc[mxu]) + widen(b2_s[...])
            second_s[slot][:, pl.ds(tile * TILE, TILE)] = jnp.tanh(out).astype(bf16)

        return finish

    def layer3(plane, slot, tile):
        mxu = tile % 2
        pltpu.matmul_push_rhs(second_s[slot][:, pl.ds(tile * TILE, TILE)], 0, mxu)
        pltpu.matmul_acc_lhs(third_acc[mxu], w3_s[...], load_staged_rhs=0)

        def finish():
            out = pltpu.matmul_pop(third_acc[mxu]) + widen(b3_s[...])
            for k in range(across):
                put(plane, tile * across + k, out[:comps, k * 128 : (k + 1) * 128])

        return finish

    def stage(one=None, two=None, three=None, beside=None):
        late = []
        for pair in range(0, tiles, 2):
            now = range(pair, min(pair + 2, tiles))
            ready = []
            if one is not None:
                ready += [layer1(*one, t) for t in now]
            for finish in late:
                finish()
            late = []
            if three is not None:
                ready += [layer3(*three, t) for t in now]
            if two is not None:
                late = [layer2(two, t) for t in now]
            for finish in ready:
                finish()
            if beside is not None:
                beside(pair // 2, (tiles + 1) // 2)
        for finish in late:
            finish()

    return stage


def accumulators(body):
    spaces = []
    for rows in (TILE, TILE, 16):
        spaces += [pltpu.ACC(mxu_id=m)((rows, TILE), f32) for m in range(2)]

    def inner(a0, a1, b0, b1, c0, c1):
        body(((a0, a1), (b0, b1), (c0, c1)))

    pl.run_scoped(inner, *spaces)


def chemistry_kernel(
    section, w1t, b1, w2, b2, w3, b3, out, cells, held, w1_s, b2_s, w3_s, b3_s, first_0, first_1, second_0, second_1, load_sem, store_sem,
    *, start, planes,
):
    first_s, second_s = (first_0, first_1), (second_0, second_1)
    comps, _, rows_y, _ = section.shape

    def load(i):
        return pltpu.make_async_copy(
            section.at[:, pl.ds(start + i, 1)], cells.at[:, pl.ds(i, 1)], load_sem.at[i]
        )

    def store(i):
        return pltpu.make_async_copy(
            held.at[:, pl.ds(i, 1)], out.at[:, pl.ds(i, 1)], store_sem.at[i]
        )

    for i in range(planes):
        load(i).start()
    prepare_weights(w1t, b1, w2, b2, w3, b3, w1_s, b2_s, w3_s, b3_s)
    flat = cells.reshape(comps * planes * rows_y, 128)
    held_flat = held.reshape(comps * planes * rows_y, 128)

    def put(plane, row, value):
        held_flat[pl.ds(plane * rows_y + row, comps, stride=planes * rows_y), :] = value

    def body(accs):
        stage = regression_stages(
            flat, comps, planes, rows_y, w1_s, w2, b2_s, w3_s, b3_s, first_s, second_s, accs, put
        )
        load(0).wait()
        stage(one=(0, 0))
        load(1).wait()
        stage(one=(rows_y, 1), two=0)

        def step(pair, carry):
            for odd in range(2):
                i = 2 * pair + odd
                load(i).wait()
                stage(one=(i * rows_y, odd), two=1 - odd, three=(i - 2, odd))
                store(i - 2).start()
            return carry

        lax.fori_loop(1, planes // 2, step, 0)
        last = planes - 1
        stage(two=last % 2, three=(last - 1, (last - 1) % 2))
        store(last - 1).start()
        stage(three=(last, last % 2))
        store(last).start()

    accumulators(body)
    for i in range(planes):
        store(i).wait()


def section_kernel(
    section, base, velocity, diffusivity, chem_in, from_low_x, from_high_x, *refs, planes, places
):
    parts = refs[: len(places)]
    (
        w1t, b1, w2, b2, w3, b3, out,
        cells, base_s, vel_s, diff_s, chem_s, out_s, w1_s, b2_s, w3_s, b3_s,
        first_0, first_1, second_0, second_1, place_s,
        cell_sem, base_sem, vel_sem, diff_sem, chem_sem, edge_sem, store_sem,
    ) = refs[len(places) : len(places) + 29]
    held_parts = refs[len(places) + 29 : -1]
    part_sem = refs[-1]
    first_s, second_s = (first_0, first_1), (second_0, second_1)
    comps, all_planes, rows_y, depth = section.shape
    stride = (all_planes + 2) * rows_y
    slots = parts[0].shape[1] - places[0]
    count = len(places) * slots
    low_y, high_y = held_parts[1], held_parts[2]

    def load_cells(x):
        return pltpu.make_async_copy(
            section.at[:, pl.ds(x, 1)], cells.at[:, pl.ds(x + 1, 1)], cell_sem.at[x]
        )

    def load_rest(x):
        one = pl.ds(x, 1)
        return [
            pltpu.make_async_copy(base.at[:, one], base_s.at[:, one], base_sem.at[x]),
            pltpu.make_async_copy(velocity.at[:, one], vel_s.at[:, one], vel_sem.at[x]),
            pltpu.make_async_copy(diffusivity.at[one], diff_s.at[one], diff_sem.at[x]),
        ]

    def load_chem(x):
        return pltpu.make_async_copy(
            chem_in.at[:, pl.ds(x - planes, 1)], chem_s.at[:, pl.ds(x, 1)], chem_sem.at[x - planes]
        )

    def store(x):
        return pltpu.make_async_copy(
            out_s.at[:, pl.ds(x, 1)], out.at[:, pl.ds(x, 1)], store_sem.at[x]
        )

    edges = [
        pltpu.make_async_copy(from_low_x, cells.at[:, 0], edge_sem.at[0]),
        pltpu.make_async_copy(from_high_x, cells.at[:, all_planes + 1], edge_sem.at[1]),
    ]
    coming = [
        pltpu.make_async_copy(part, held, part_sem.at[k])
        for k, (part, held) in enumerate(zip(parts, held_parts))
    ]
    spray_planes = SB // rows_y

    load_cells(0).start()
    load_cells(planes - 1).start()
    load_cells(planes).start()
    load_cells(planes + 1).start()
    for copy in coming:
        copy.start()
    for x in range(spray_planes):
        load_rest(x)[0].start()
    for x in range(planes):
        if x + 1 < planes - 1:
            load_cells(x + 1).start()
        if planes + x + 2 < all_planes:
            load_cells(planes + x + 2).start()
        load_chem(planes + x).start()
        for copy in load_rest(planes + x):
            copy.start()
        for copy in load_rest(x)[x < spray_planes :]:
            copy.start()
        if x == 1:
            for copy in edges:
                copy.start()
    prepare_weights(w1t, b1, w2, b2, w3, b3, w1_s, b2_s, w3_s, b3_s)

    flat = cells.reshape(comps * stride, 128)
    chem_flat = chem_s.reshape(comps * all_planes * rows_y, 128)

    def put(plane, row, value):
        chem_flat[pl.ds(plane * rows_y + row, comps, stride=all_planes * rows_y), :] = value

    row_id = lax.broadcasted_iota(jnp.int32, (rows_y, depth), 0)
    lane_id = lax.broadcasted_iota(jnp.int32, (rows_y, depth), 1)

    def coefficients(x):
        spread = scale * diff_s[x]
        half = [(0.5 * scale) * vel_s[d, x] for d in range(3)]
        up = [spread - h for h in half]
        down = [spread + h for h in half]
        up[2] = jnp.where(lane_id == depth - 1, 0.0, up[2])
        down[2] = jnp.where(lane_id == 0, 0.0, down[2])
        return up, down, keep_section - 6.0 * spread

    def combine(x, comp, up, down, middle):
        center = cells[comp, x + 1]
        above_y = jnp.broadcast_to(high_y[comp, pl.ds(x, 1), :], (rows_y, depth))
        below_y = jnp.broadcast_to(low_y[comp, pl.ds(x, 1), :], (rows_y, depth))
        plus_y = jnp.where(row_id == rows_y - 1, above_y, pltpu.roll(center, rows_y - 1, 0))
        minus_y = jnp.where(row_id == 0, below_y, pltpu.roll(center, 1, 0))
        total = keep_base * base_s[comp, x] + middle * center
        total += up[0] * cells[comp, x + 2] + down[0] * cells[comp, x]
        total += up[1] * plus_y + down[1] * minus_y
        total += up[2] * pltpu.roll(center, depth - 1, 1) + down[2] * pltpu.roll(center, 1, 1)
        out_s[comp, x] = total + scale * chem_s[comp, x]

    def update(x, part=0, pieces=1):
        up, down, middle = coefficients(x)
        for comp in range(part * comps // pieces, (part + 1) * comps // pieces):
            combine(x, comp, up, down, middle)

    def deposit(first_acc):
        tags = jnp.concatenate(
            [held[comps, pl.ds(row, slots)] for held, row in zip(held_parts, places)], axis=0
        )
        lanes = lax.broadcasted_iota(jnp.int32, tags.shape, 1).astype(f32)
        chosen = jnp.transpose((tags - 1.0 == lanes).astype(f32))
        place_s[...] = jnp.zeros(place_s.shape, bf16)
        place_s[:SB, :count] = chosen[:SB].astype(bf16)
        for comp in range(0, comps, 2):
            mxu = (comp // 2) % 2
            pair = [
                jnp.concatenate(
                    [held[comp + k, pl.ds(row, slots)] for held, row in zip(held_parts, places)],
                    axis=0,
                )
                for k in range(2)
            ]
            block = jnp.concatenate(pair, axis=1).astype(bf16)
            block = jnp.concatenate([block, jnp.zeros((TILE - count, TILE), bf16)], axis=0)
            pltpu.matmul_push_rhs(block, 0, mxu)
            pltpu.matmul_acc_lhs(first_acc[mxu], place_s[...], load_staged_rhs=0)
            mine = pltpu.matmul_pop(first_acc[mxu])[:SB]
            for k in range(2):
                piece = mine[:, k * 128 : (k + 1) * 128].reshape(spray_planes, rows_y, depth)
                base_s[comp + k, :spray_planes] += (scale / keep_base) * piece

    def body(accs):
        stage = regression_stages(
            flat, comps, planes, rows_y, w1_s, w2, b2_s, w3_s, b3_s, first_s, second_s, accs, put
        )

        def far_ready(i):
            @pl.when(i < planes - 1)
            def _():
                load_cells(planes + i + 1).wait()

            load_chem(planes + i).wait()
            for copy in load_rest(planes + i):
                copy.wait()

        def near_ready(i):
            for copy in load_rest(i)[1:]:
                copy.wait()

            @pl.when(i >= spray_planes)
            def _():
                load_rest(i)[0].wait()

        def run(i, near, **layers):
            far_ready(i)
            if near is not None:
                near_ready(near)

            def beside(part, pieces):
                if near is None:
                    update(planes + i, part, pieces)
                elif part < pieces // 2:
                    update(planes + i, part, pieces // 2)
                else:
                    update(near, part - pieces // 2, pieces - pieces // 2)

            stage(beside=beside, **layers)
            store(planes + i).start()
            if near is not None:
                store(near).start()

        load_cells(0).wait()
        load_cells(planes - 1).wait()
        load_cells(planes).wait()
        for copy in coming:
            copy.wait()
        for x in range(spray_planes):
            load_rest(x)[0].wait()
        deposit(accs[0])
        for copy in edges:
            copy.wait()

        run(0, None, one=(rows_y, 0))
        load_cells(1).wait()
        run(1, None, one=(2 * rows_y, 1), two=0)
        load_cells(2).wait()
        run(2, None, one=(3 * rows_y, 0), two=1, three=(0, 0))
        load_cells(3).wait()
        run(3, 0, one=(4 * rows_y, 1), two=0, three=(1, 1))

        def step(pair, carry):
            for odd in range(2):
                i = 2 * pair + odd

                @pl.when(i < planes - 1)
                def _():
                    load_cells(i).wait()

                run(i, i - 3, one=((i + 1) * rows_y, odd), two=1 - odd, three=(i - 2, odd))
            return carry

        lax.fori_loop(2, planes // 2, step, 0)
        last = planes - 1
        near_ready(last - 2)
        stage(
            two=last % 2,
            three=(last - 1, (last - 1) % 2),
            beside=functools.partial(update, last - 2),
        )
        store(last - 2).start()
        near_ready(last - 1)
        stage(three=(last, last % 2), beside=functools.partial(update, last - 1))
        store(last - 1).start()
        near_ready(last)
        update(last)
        store(last).start()

    accumulators(body)
    for x in range(all_planes):
        store(x).wait()


def faces_kernel(owner, block, projected, section, low_x, high_x, *refs, shifts):
    sends, (lower, upper, sems) = refs[:-3], refs[-3:]
    comps, planes, rows_y, depth = section.shape
    edge = lower.shape[2]
    count = projected.shape[1]
    tiles_y = len(shifts)
    capacity = sends[0].shape[1]
    me = lax.axis_index("gy")
    copies = [
        pltpu.make_async_copy(section.at[:, :, pl.ds(0, edge)], lower, sems.at[0]),
        pltpu.make_async_copy(section.at[:, :, pl.ds(rows_y - edge, edge)], upper, sems.at[1]),
        pltpu.make_async_copy(section.at[:, 0], low_x, sems.at[2]),
        pltpu.make_async_copy(section.at[:, planes - 1], high_x, sems.at[3]),
    ]
    for copy in copies:
        copy.start()
    own = owner[...]
    some = -(-tiles_y // 8) * 8
    hits = (lax.broadcasted_iota(jnp.int32, (some, count), 0) == own).astype(f32)
    before = lax.broadcasted_iota(jnp.int32, (count, count), 0) < lax.broadcasted_iota(
        jnp.int32, (count, count), 1
    )
    counts = jnp.dot(
        hits.astype(bf16), before.astype(f32).astype(bf16), preferred_element_type=f32
    )
    rank = jnp.sum(counts * hits, axis=0, keepdims=True).astype(jnp.int32)
    order = jnp.zeros_like(own)
    for k, shift in enumerate(shifts):
        order = jnp.where(own == lax.rem(me + shift, tiles_y), k, order)
    slot = order * capacity + rank
    chosen = lax.broadcasted_iota(jnp.int32, (tiles_y * capacity, count), 0) == slot
    numbers = jnp.sum(
        jnp.where(chosen, (block[...] + 1).astype(f32), 0.0), axis=1, keepdims=True
    )
    numbers = jnp.broadcast_to(numbers, (tiles_y * capacity, depth))
    picked = chosen.astype(f32).astype(bf16)

    def put(comp, value):
        for k, send in enumerate(sends):
            rows = pl.ds(send.shape[1] - capacity, capacity)
            send[comp, rows] = value[k * capacity : (k + 1) * capacity]

    for comp in range(comps):
        put(comp, jnp.dot(picked, projected[comp], preferred_element_type=f32))
    put(comps, numbers)
    for copy in copies:
        copy.wait()
    for send, held, row, last in (
        (sends[1], upper, edge - 1, me == tiles_y - 1),
        (sends[2], lower, 0, me == 0),
    ):
        lines = held.reshape(comps * planes * edge, depth)
        layer = lines[pl.ds(row, comps * planes, stride=edge), :]
        layer = jnp.where(last, 0.0, layer)
        for comp in range(comps):
            send[comp, pl.ds(0, planes)] = layer[comp * planes : (comp + 1) * planes]
        send[comps, pl.ds(0, planes)] = jnp.zeros((planes, depth), f32)


def shards(
    base_scores,
    section_scores,
    velocity,
    diffusivity,
    w_first,
    b_first,
    w_second,
    b_second,
    w_third,
    b_third,
    loadings,
    parcel_species,
    parcel_owner,
    parcel_block,
):
    comps, rows_x, rows_y, depth = section_scores.shape
    hidden = w_second.shape[0]
    blocks_here = parcel_species.shape[0]
    tiles_y = lax.axis_size("gy")
    capacity = max(2, 2 * blocks_here // tiles_y)
    planes = rows_x // 2
    rest = rows_x - planes
    whole = pl.BlockSpec(memory_space=pltpu.VMEM)
    anywhere = pl.BlockSpec(memory_space=pltpu.HBM)
    sems = pltpu.SemaphoreType.DMA
    params = pltpu.CompilerParams(vmem_limit_bytes=60 * 2**20)

    projected = jnp.einsum(
        "ks,psc->kpc", loadings, parcel_species, preferred_element_type=f32
    ).astype(bf16)
    shifts = [0, 1, tiles_y - 1] + list(range(2, tiles_y - 1))
    faces = [0, rows_x, rows_x] + [0] * (tiles_y - 3)
    face_x = jax.ShapeDtypeStruct((comps, rows_y, depth), f32)
    low_x, high_x, *sends = pl.pallas_call(
        functools.partial(faces_kernel, shifts=shifts),
        in_specs=[whole] * 3 + [anywhere],
        out_specs=[whole] * (2 + tiles_y),
        out_shape=[face_x] * 2
        + [jax.ShapeDtypeStruct((comps + 1, face + capacity, depth), f32) for face in faces],
        scratch_shapes=[pltpu.VMEM((comps, rows_x, 8, depth), f32)] * 2 + [sems((4,))],
        compiler_params=params,
    )(parcel_owner.reshape(1, -1), parcel_block.reshape(1, -1), projected, section_scores)

    tiles_x = lax.axis_size("gx")
    forward = [(i, i + 1) for i in range(tiles_x - 1)]
    backward = [(target, source) for source, target in forward]
    from_low_x = lax.ppermute(high_x, "gx", forward)
    from_high_x = lax.ppermute(low_x, "gx", backward)
    parts = [sends[0]] + [
        lax.ppermute(send, "gy", [(i, (i + shift) % tiles_y) for i in range(tiles_y)])
        for send, shift in zip(sends[1:], shifts[1:])
    ]

    weights = (
        w_first.T,
        b_first.reshape(1, -1),
        w_second,
        b_second.reshape(1, -1),
        w_third,
        b_third.reshape(1, -1),
    )
    prepared = [
        pltpu.VMEM((hidden, TILE), bf16),
        pltpu.VMEM((hidden, 128), f32),
        pltpu.VMEM((16, hidden), bf16),
        pltpu.VMEM((16, 128), f32),
    ] + [pltpu.VMEM((hidden, rows_y * depth), bf16)] * 4
    per_plane = 2 * rows_y * depth * hidden * (2 * comps + hidden)
    chem = pl.pallas_call(
        functools.partial(chemistry_kernel, start=planes, planes=rest),
        in_specs=[anywhere] + [whole] * 6,
        out_specs=anywhere,
        out_shape=jax.ShapeDtypeStruct((comps, rest, rows_y, depth), f32),
        scratch_shapes=[pltpu.VMEM((comps, rest, rows_y, depth), f32)] * 2
        + prepared
        + [sems((rest,)), sems((rest,))],
        compiler_params=params,
        cost_estimate=pl.CostEstimate(
            flops=rest * per_plane,
            bytes_accessed=8 * comps * rest * rows_y * depth,
            transcendentals=2 * hidden * rest * rows_y * depth,
        ),
    )(section_scores, *weights)
    tile = (comps, rows_x, rows_y, depth)
    return pl.pallas_call(
        functools.partial(section_kernel, planes=planes, places=faces),
        in_specs=[anywhere] * 5
        + [pl.BlockSpec(memory_space=pl.ANY)] * (2 + len(parts))
        + [whole] * 6,
        out_specs=anywhere,
        out_shape=jax.ShapeDtypeStruct(tile, f32),
        scratch_shapes=[
            pltpu.VMEM((comps, rows_x + 2, rows_y, depth), f32),
            pltpu.VMEM(tile, f32),
            pltpu.VMEM((3, rows_x, rows_y, depth), f32),
            pltpu.VMEM((rows_x, rows_y, depth), f32),
            pltpu.VMEM(tile, f32),
            pltpu.VMEM(tile, f32),
        ]
        + prepared
        + [pltpu.VMEM((TILE, TILE), bf16)]
        + [sems((rows_x,))] * 4
        + [sems((rest,)), sems((2,)), sems((rows_x,))]
        + [pltpu.VMEM(part.shape, f32) for part in parts]
        + [sems((len(parts),))],
        compiler_params=params,
        cost_estimate=pl.CostEstimate(
            flops=planes * per_plane,
            bytes_accessed=16 * comps * rows_x * rows_y * depth,
            transcendentals=2 * hidden * planes * rows_y * depth,
        ),
    )(
        section_scores, base_scores, velocity, diffusivity, chem, from_low_x, from_high_x,
        *parts, *weights,
    )


def solution(mesh):
    placed = (
        P(None, "gx", "gy", None),
        P(None, "gx", "gy", None),
        P(None, "gx", "gy", None),
        P("gx", "gy", None),
        P(),
        P(),
        P(),
        P(),
        P(),
        P(),
        P(),
        P(("gx", "gy"), None, None),
        P(("gx", "gy"), None),
        P(("gx", "gy")),
    )
    return jax.shard_map(
        shards, mesh=mesh, in_specs=placed, out_specs=P(None, "gx", "gy", None), check_vma=False
    )
```

time: 162 us -> 59.7 us (0.37)
  the two profiles are of different devices: /device:TPU:25 before, /device:TPU:8 now
where the time goes in v2:
time: 59.7 us; the launch traced here: 59.4 us
  Pallas kernels  44.5 us (75%)
  starting transfers between devices  10 us (17%)
  local copies, waits for them, and re-layouts  3.23 us (5%)
  matrix products  1.5 us (3%)
    pallas_call x1, Pallas kernels, shards(): pl.pallas_call(functools.partial(section_kernel, planes=planes, places=fa...  23.8 us
    pallas_call x1, Pallas kernels, shards(): pl.pallas_call(functools.partial(chemistry_kernel, start=planes, planes=r...  16.9 us
    pallas_call x1, Pallas kernels, shards(): pl.pallas_call(functools.partial(faces_kernel, shifts=shifts), in_specs=[...  3.83 us
    ppermute x1, starting transfers between devices, shards(): from_low_x = lax.ppermute(high_x, 'gx', forward)  3.43 us
    ppermute x1, starting transfers between devices, shards(): from_high_x = lax.ppermute(low_x, 'gx', backward)  3.31 us
    ppermute x3, starting transfers between devices, shards(): lax.ppermute(send, 'gy', [(i, (i + shift) % tiles_y) for i in range(tiles...  3.3 us
    unnamed x12, local copies, waits for them, and re-layouts  2.55 us
    dot_general x1, matrix products, shards(): jnp.einsum('ks,psc->kpc', loadings, parcel_species, preferred_element_typ...  1.5 us
  transfers between devices with their start and end apart: 5, of which 0 were waited for; matrix products, arithmetic and copies ran while one was open for 0% of the time, Pallas kernels for 28%

profile of v2, /device:TPU:8, one launch (start us, length us, event | category | flops | bytes accessed | tf_op | source)
XLA Modules:
  0.0 59.4 jit_solution(11094830953833794677)
XLA Ops:
  0.0 0.0 copy-start
  0.0 1.7 %copy-done = bf16[32,300,128]{2,0,1:T(8,128)(2,1)S(1)} copy-done((bf16[32,300,128]{2,0,1:T(8,128)(2,1)S(1)}, bf16[32,300,128]{2,0,1:T(8,128)(2,1)}, u32[]{:S(2)}) %copy-start) | copy-done | bytes 2457624
  1.7 1.5 %fusion = bf16[12,32,128]{2,0,1:T(8,128)(2,1)S(1)} fusion(bf16[32,300,128]{2,0,1:T(8,128)(2,1)S(1)} %copy-done, bf16[12,300]{1,0:T(8,128)(2,1)} %param.24), kind=kOutput, calls=%fused_computation | convolution fusion | flops 29491200 | bytes 2563104 | tf_op jit(solution)/shard_map/ks,psc->kpc/dot_general | solution.py:504
  3.2 0.7 %copy.20.projected = bf16[12,32,128]{2,1,0:T(8,128)(2,1)} copy(bf16[12,32,128]{2,0,1:T(8,128)(2,1)S(1)} %fusion) | data formatting | bytes 196608 | tf_op jit(solution)/shard_map/ks,psc->kpc/dot_general | solution.py:504
  3.9 3.8 %shard_map.137 = (f32[12,16,128]{2,1,0:T(8,128)}, f32[12,16,128]{2,1,0:T(8,128)}, f32[13,16,128]{2,1,0:T(8,128)}, f32[13,48,128]{2,1,0:T(8,128)}, f32[13,48,128]{2,1,0:T(8,128)}, /*index=5*/f32[13,16,128]{2,1,0:T(8,128)}) custom-call(s32[1,32]{1,0:T(1,128)} %bitcast.9, s32[1,32]{1,0:T(1,128)} %bitcast.10, bf16[12,32,128]{2,1,0:T(8,128)(2,1)} %copy.20.projected, ...), custom_call_target="tpu_custom_call" | custom-call | tf_op jit(solution)/shard_map/pallas_call | solution.py:510
  7.7 3.4 %collective-permute-start = (f32[12,16,128]{2,1,0:T(8,128)}, f32[12,16,128]{2,1,0:T(8,128)S(1)}, u32[]{:S(2)}, u32[]{:S(2)}) collective-permute-start(f32[12,16,128]{2,1,0:T(8,128)} %get-tuple-element.11), channel_id=1, source_target_pairs={{0,4},{4,8},{8,12},{12,16},{16,20},{20,24},{24,28},{1,5},{5,9},{9,... | collective-permute-start | bytes 294920 | tf_op jit(solution)/shard_map/ppermute | solution.py:523
  11.1 3.3 %collective-permute-start.1 = (f32[12,16,128]{2,1,0:T(8,128)}, f32[12,16,128]{2,1,0:T(8,128)S(1)}, u32[]{:S(2)}, u32[]{:S(2)}) collective-permute-start(f32[12,16,128]{2,1,0:T(8,128)} %get-tuple-element.12), channel_id=1, source_target_pairs={{4,0},{8,4},{12,8},{16,12},{20,16},{24,20},{28,24},{5,1},{9,5},{13... | collective-permute-start | bytes 294920 | tf_op jit(solution)/shard_map/ppermute | solution.py:524
  14.5 1.6 %collective-permute-start.4 = (f32[13,16,128]{2,1,0:T(8,128)}, f32[13,16,128]{2,1,0:T(8,128)S(1)}, u32[]{:S(2)}, u32[]{:S(2)}) collective-permute-start(f32[13,16,128]{2,1,0:T(8,128)} %get-tuple-element.16), channel_id=1, source_target_pairs={{0,2},{1,3},{2,0},{3,1},{4,6},{5,7},{6,4},{7,5},{8,10},{9,11},{10,... | collective-permute-start | bytes 319496 | tf_op jit(solution)/shard_map/ppermute | solution.py:526
  16.0 0.0 collective-permute-start.2
  16.0 1.7 %collective-permute-start.3 = (f32[13,48,128]{2,1,0:T(8,128)}, f32[13,48,128]{2,1,0:T(8,128)S(1)}, u32[]{:S(2)}, u32[]{:S(2)}) collective-permute-start(f32[13,48,128]{2,1,0:T(8,128)} %get-tuple-element.15), channel_id=1, source_target_pairs={{0,3},{1,0},{2,1},{3,2},{4,7},{5,4},{6,5},{7,6},{8,11},{9,8},{10,9... | collective-permute-start | bytes 958472 | tf_op jit(solution)/shard_map/ppermute | solution.py:526
  17.8 16.9 %shard_map.136.chem_in = f32[12,16,16,128]{3,2,1,0:T(8,128)} custom-call(f32[12,32,16,128]{3,2,1,0:T(8,128)} %section.5, bf16[12,256]{1,0:T(8,128)(2,1)} %bitcast.11, f32[1,256]{1,0:T(1,128)} %bitcast.13, bf16[256,256]{1,0:T(8,128)(2,1)} %refs_6_.1, f32[1,256]{1,0:T(1,128)} %bitcast.15, bf16[12,256]{1,0:T(8,128)(2,1)} %refs_8_.1, f32[1,12]{1,0:T(1,128)} %bitcast.17), custom_call_target="tpu_custom_call" | custom-call | flops 4697620480 | bytes 3145728 | tf_op jit(solution)/shard_map/pallas_call | solution.py:545
  34.6 0.0 collective-permute-done.from_low_x
  34.6 0.0 copy-start.4
  34.7 0.0 collective-permute-done.1.from_high_x
  34.7 0.0 copy-start.5
  34.7 0.0 collective-permute-done.4.refs_3_
  34.7 0.0 copy-start.3
  34.7 0.0 collective-permute-done.2.refs_1_
  34.7 0.0 copy-start.1
  34.7 0.0 collective-permute-done.3.refs_2_
  34.7 0.0 copy-start.2
  34.7 0.5 copy-done.4
  35.3 0.0 copy-done.5
  35.3 0.0 copy-done.3
  35.4 0.1 copy-done.1
  35.5 0.1 copy-done.2
  35.6 23.8 %shard_map.138 = f32[12,32,16,128]{3,2,1,0:T(8,128)} custom-call(f32[12,32,16,128]{3,2,1,0:T(8,128)} %section.5, f32[12,32,16,128]{3,2,1,0:T(8,128)} %base.1, f32[3,32,16,128]{3,2,1,0:T(8,128)} %velocity.1, f32[32,16,128]{2,1,0:T(8,128)} %diffusivity.1, f32[12,16,16,128]{3,2,1,0:T(8,128)} %shard_map.136.chem_in, f32[12,16,128]{2,1,0:T(8,128)} %copy-done.4, ...), custom_call_target="tpu_custom_call" | custom-call | flops 4697620480 | bytes 12582912 | tf_op jit(solution)/shard_map/pallas_call | solution.py:561
Async XLA Ops:
  0.0 1.7 %copy-start = (bf16[32,300,128]{2,0,1:T(8,128)(2,1)S(1)}, bf16[32,300,128]{2,0,1:T(8,128)(2,1)}, u32[]{:S(2)}) copy-start(bf16[32,300,128]{2,0,1:T(8,128)(2,1)} %param.25) | copy-start | bytes 7372804
  7.7 26.9 %collective-permute-start = (f32[12,16,128]{2,1,0:T(8,128)}, f32[12,16,128]{2,1,0:T(8,128)S(1)}, u32[]{:S(2)}, u32[]{:S(2)}) collective-permute-start(f32[12,16,128]{2,1,0:T(8,128)} %get-tuple-element.11), channel_id=1, source_target_pairs={{0,4},{4,8},{8,12},{12,16},{16,20},{20,24},{24,28},{1,5},{5,9},{9,... | collective-permute-start | bytes 294920 | tf_op jit(solution)/shard_map/ppermute | solution.py:523
  11.1 23.5 %collective-permute-start.1 = (f32[12,16,128]{2,1,0:T(8,128)}, f32[12,16,128]{2,1,0:T(8,128)S(1)}, u32[]{:S(2)}, u32[]{:S(2)}) collective-permute-start(f32[12,16,128]{2,1,0:T(8,128)} %get-tuple-element.12), channel_id=1, source_target_pairs={{4,0},{8,4},{12,8},{16,12},{20,16},{24,20},{28,24},{5,1},{9,5},{13... | collective-permute-start | bytes 294920 | tf_op jit(solution)/shard_map/ppermute | solution.py:524
  14.5 20.2 %collective-permute-start.4 = (f32[13,16,128]{2,1,0:T(8,128)}, f32[13,16,128]{2,1,0:T(8,128)S(1)}, u32[]{:S(2)}, u32[]{:S(2)}) collective-permute-start(f32[13,16,128]{2,1,0:T(8,128)} %get-tuple-element.16), channel_id=1, source_target_pairs={{0,2},{1,3},{2,0},{3,1},{4,6},{5,7},{6,4},{7,5},{8,10},{9,11},{10,... | collective-permute-start | bytes 319496 | tf_op jit(solution)/shard_map/ppermute | solution.py:526
  16.0 18.7 %collective-permute-start.2 = (f32[13,48,128]{2,1,0:T(8,128)}, f32[13,48,128]{2,1,0:T(8,128)S(1)}, u32[]{:S(2)}, u32[]{:S(2)}) collective-permute-start(f32[13,48,128]{2,1,0:T(8,128)} %get-tuple-element.14), channel_id=1, source_target_pairs={{0,1},{1,2},{2,3},{3,0},{4,5},{5,6},{6,7},{7,4},{8,9},{9,10},{10,1... | collective-permute-start | bytes 958472 | tf_op jit(solution)/shard_map/ppermute | solution.py:526
  16.0 18.7 %collective-permute-start.3 = (f32[13,48,128]{2,1,0:T(8,128)}, f32[13,48,128]{2,1,0:T(8,128)S(1)}, u32[]{:S(2)}, u32[]{:S(2)}) collective-permute-start(f32[13,48,128]{2,1,0:T(8,128)} %get-tuple-element.15), channel_id=1, source_target_pairs={{0,3},{1,0},{2,1},{3,2},{4,7},{5,4},{6,5},{7,6},{8,11},{9,8},{10,9... | collective-permute-start | bytes 958472 | tf_op jit(solution)/shard_map/ppermute | solution.py:526
  34.6 0.6 %copy-start.4 = (f32[12,16,128]{2,1,0:T(8,128)}, f32[12,16,128]{2,1,0:T(8,128)S(1)}, u32[]{:S(2)}) copy-start(f32[12,16,128]{2,1,0:T(8,128)S(1)} %collective-permute-done.from_low_x) | copy-start | bytes 294916
  34.7 0.7 %copy-start.5 = (f32[12,16,128]{2,1,0:T(8,128)}, f32[12,16,128]{2,1,0:T(8,128)S(1)}, u32[]{:S(2)}) copy-start(f32[12,16,128]{2,1,0:T(8,128)S(1)} %collective-permute-done.1.from_high_x) | copy-start | bytes 294916
  34.7 0.7 %copy-start.3 = (f32[13,16,128]{2,1,0:T(8,128)}, f32[13,16,128]{2,1,0:T(8,128)S(1)}, u32[]{:S(2)}) copy-start(f32[13,16,128]{2,1,0:T(8,128)S(1)} %collective-permute-done.4.refs_3_) | copy-start | bytes 319492
  34.7 0.8 %copy-start.1 = (f32[13,48,128]{2,1,0:T(8,128)}, f32[13,48,128]{2,1,0:T(8,128)S(1)}, u32[]{:S(2)}) copy-start(f32[13,48,128]{2,1,0:T(8,128)S(1)} %collective-permute-done.2.refs_1_) | copy-start | bytes 958468
  34.7 0.9 %copy-start.2 = (f32[13,48,128]{2,1,0:T(8,128)}, f32[13,48,128]{2,1,0:T(8,128)S(1)}, u32[]{:S(2)}) copy-start(f32[13,48,128]{2,1,0:T(8,128)S(1)} %collective-permute-done.3.refs_2_) | copy-start | bytes 958468

commit v3 on v2

--- a/solution.py
+++ b/solution.py
@@ -1,4 +1,5 @@
 import functools
+import math
 
 import jax
 import jax.numpy as jnp
@@ -22,7 +23,15 @@
     return jnp.transpose(jnp.broadcast_to(row, (width, row.shape[1])))
 
 
-def prepare_weights(w1t, b1, w2, b2, w3, b3, w1_s, b2_s, w3_s, b3_s):
+def weight_copies(weights, held, sems):
+    return [
+        pltpu.make_async_copy(weight, place, sems.at[k])
+        for k, (weight, place) in enumerate(zip(weights, held))
+    ]
+
+
+def prepare_weights(held, w1_s, b2_s, w3_s, b3_s):
+    w1t, b1, _, b2, w3, b3 = held
     comps, hidden = w1t.shape
     bias = b1[...]
     high = bias.astype(bf16).astype(f32)
@@ -132,16 +141,21 @@
     pl.run_scoped(inner, *spaces)
 
 
-def chemistry_kernel(
-    section, w1t, b1, w2, b2, w3, b3, out, cells, held, w1_s, b2_s, w3_s, b3_s, first_0, first_1, second_0, second_1, load_sem, store_sem,
-    *, start, planes,
-):
-    first_s, second_s = (first_0, first_1), (second_0, second_1)
+def chemistry_kernel(section, *refs, start, planes, chunk):
+    weights, out, refs = refs[:6], refs[6], refs[7:]
+    (cells, held, w1_s, b2_s, w3_s, b3_s, first_0, first_1, second_0, second_1), refs = (
+        refs[:10],
+        refs[10:],
+    )
+    weights_s, (load_sem, store_sem, weight_sem) = refs[:6], refs[6:]
+    first_s, second_s, w2 = (first_0, first_1), (second_0, second_1), weights_s[2]
     comps, _, rows_y, _ = section.shape
 
-    def load(i):
+    def load(k):
         return pltpu.make_async_copy(
-            section.at[:, pl.ds(start + i, 1)], cells.at[:, pl.ds(i, 1)], load_sem.at[i]
+            section.at[:, pl.ds(start + k * chunk, chunk)],
+            cells.at[:, pl.ds(k * chunk, chunk)],
+            load_sem.at[k],
         )
 
     def store(i):
@@ -149,9 +163,15 @@
             held.at[:, pl.ds(i, 1)], out.at[:, pl.ds(i, 1)], store_sem.at[i]
         )
 
-    for i in range(planes):
-        load(i).start()
-    prepare_weights(w1t, b1, w2, b2, w3, b3, w1_s, b2_s, w3_s, b3_s)
+    load(0).start()
+    copies = weight_copies(weights, weights_s, weight_sem)
+    for copy in copies:
+        copy.start()
+    for k in range(1, planes // chunk):
+        load(k).start()
+    for copy in copies:
+        copy.wait()
+    prepare_weights(weights_s, w1_s, b2_s, w3_s, b3_s)
     flat = cells.reshape(comps * planes * rows_y, 128)
     held_flat = held.reshape(comps * planes * rows_y, 128)
 
@@ -162,20 +182,23 @@
         stage = regression_stages(
             flat, comps, planes, rows_y, w1_s, w2, b2_s, w3_s, b3_s, first_s, second_s, accs, put
         )
+        def run(i, odd):
+            stage(one=(i * rows_y, odd), two=1 - odd, three=(i - 2, odd))
+            store(i - 2).start()
+
         load(0).wait()
         stage(one=(0, 0))
-        load(1).wait()
         stage(one=(rows_y, 1), two=0)
-
-        def step(pair, carry):
-            for odd in range(2):
-                i = 2 * pair + odd
-                load(i).wait()
-                stage(one=(i * rows_y, odd), two=1 - odd, three=(i - 2, odd))
-                store(i - 2).start()
+        for i in range(2, chunk):
+            run(i, i % 2)
+
+        def step(k, carry):
+            load(k).wait()
+            for j in range(chunk):
+                run(k * chunk + j, j % 2)
             return carry
 
-        lax.fori_loop(1, planes // 2, step, 0)
+        lax.fori_loop(1, planes // chunk, step, 0)
         last = planes - 1
         stage(two=last % 2, three=(last - 1, (last - 1) % 2))
         store(last - 1).start()
@@ -187,41 +210,46 @@
         store(i).wait()
 
 
-def section_kernel(
-    section, base, velocity, diffusivity, chem_in, from_low_x, from_high_x, *refs, planes, places
-):
-    parts = refs[: len(places)]
-    (
-        w1t, b1, w2, b2, w3, b3, out,
-        cells, base_s, vel_s, diff_s, chem_s, out_s, w1_s, b2_s, w3_s, b3_s,
-        first_0, first_1, second_0, second_1, place_s,
-        cell_sem, base_sem, vel_sem, diff_sem, chem_sem, edge_sem, store_sem,
-    ) = refs[len(places) : len(places) + 29]
-    held_parts = refs[len(places) + 29 : -1]
-    part_sem = refs[-1]
-    first_s, second_s = (first_0, first_1), (second_0, second_1)
+def section_kernel(section, base, velocity, diffusivity, chem_in, from_low_x, from_high_x, *refs, planes, places, chunk):
+    parts, refs = refs[: len(places)], refs[len(places) :]
+    weights, out, refs = refs[:6], refs[6], refs[7:]
+    (cells, base_s, vel_s, diff_s, chem_s, out_s, place_s), refs = refs[:7], refs[7:]
+    (w1_s, b2_s, w3_s, b3_s, first_0, first_1, second_0, second_1), refs = refs[:8], refs[8:]
+    weights_s, refs = refs[:6], refs[6:]
+    (cell_sem, base_sem, vel_sem, diff_sem, chem_sem, edge_sem, store_sem), refs = (
+        refs[:7],
+        refs[7:],
+    )
+    held_parts, (part_sem, weight_sem) = refs[: len(places)], refs[len(places) :]
+    first_s, second_s, w2 = (first_0, first_1), (second_0, second_1), weights_s[2]
     comps, all_planes, rows_y, depth = section.shape
     stride = (all_planes + 2) * rows_y
     slots = parts[0].shape[1] - places[0]
     count = len(places) * slots
     low_y, high_y = held_parts[1], held_parts[2]
-
-    def load_cells(x):
+    spray_planes = SB // rows_y
+    near_chunks = planes // chunk
+
+    def load_cells(k):
         return pltpu.make_async_copy(
-            section.at[:, pl.ds(x, 1)], cells.at[:, pl.ds(x + 1, 1)], cell_sem.at[x]
-        )
-
-    def load_rest(x):
-        one = pl.ds(x, 1)
+            section.at[:, pl.ds(k * chunk, chunk)],
+            cells.at[:, pl.ds(k * chunk + 1, chunk)],
+            cell_sem.at[k],
+        )
+
+    def load_rest(k):
+        some = pl.ds(k * chunk, chunk)
         return [
-            pltpu.make_async_copy(base.at[:, one], base_s.at[:, one], base_sem.at[x]),
-            pltpu.make_async_copy(velocity.at[:, one], vel_s.at[:, one], vel_sem.at[x]),
-            pltpu.make_async_copy(diffusivity.at[one], diff_s.at[one], diff_sem.at[x]),
+            pltpu.make_async_copy(base.at[:, some], base_s.at[:, some], base_sem.at[k]),
+            pltpu.make_async_copy(velocity.at[:, some], vel_s.at[:, some], vel_sem.at[k]),
+            pltpu.make_async_copy(diffusivity.at[some], diff_s.at[some], diff_sem.at[k]),
         ]
 
-    def load_chem(x):
+    def load_chem(k):
         return pltpu.make_async_copy(
-            chem_in.at[:, pl.ds(x - planes, 1)], chem_s.at[:, pl.ds(x, 1)], chem_sem.at[x - planes]
+            chem_in.at[:, pl.ds(k * chunk, chunk)],
+            chem_s.at[:, pl.ds(planes + k * chunk, chunk)],
+            chem_sem.at[k],
         )
 
     def store(x):
@@ -237,30 +265,24 @@
         pltpu.make_async_copy(part, held, part_sem.at[k])
         for k, (part, held) in enumerate(zip(parts, held_parts))
     ]
-    spray_planes = SB // rows_y
 
     load_cells(0).start()
-    load_cells(planes - 1).start()
-    load_cells(planes).start()
-    load_cells(planes + 1).start()
-    for copy in coming:
+    copies = weight_copies(weights, weights_s, weight_sem)
+    for copy in copies:
         copy.start()
-    for x in range(spray_planes):
-        load_rest(x)[0].start()
-    for x in range(planes):
-        if x + 1 < planes - 1:
-            load_cells(x + 1).start()
-        if planes + x + 2 < all_planes:
-            load_cells(planes + x + 2).start()
-        load_chem(planes + x).start()
-        for copy in load_rest(planes + x):
+    for k in range(near_chunks):
+        for copy in load_rest(near_chunks + k) + load_rest(k):
             copy.start()
-        for copy in load_rest(x)[x < spray_planes :]:
-            copy.start()
-        if x == 1:
-            for copy in edges:
+        load_cells(near_chunks + k).start()
+        load_chem(k).start()
+        if k == 0:
+            for copy in coming + edges:
                 copy.start()
-    prepare_weights(w1t, b1, w2, b2, w3, b3, w1_s, b2_s, w3_s, b3_s)
+        if k + 1 < near_chunks:
+            load_cells(k + 1).start()
+    for copy in copies:
+        copy.wait()
+    prepare_weights(weights_s, w1_s, b2_s, w3_s, b3_s)
 
     flat = cells.reshape(comps * stride, 128)
     chem_flat = chem_s.reshape(comps * all_planes * rows_y, 128)
@@ -328,84 +350,53 @@
             flat, comps, planes, rows_y, w1_s, w2, b2_s, w3_s, b3_s, first_s, second_s, accs, put
         )
 
-        def far_ready(i):
-            @pl.when(i < planes - 1)
-            def _():
-                load_cells(planes + i + 1).wait()
-
-            load_chem(planes + i).wait()
-            for copy in load_rest(planes + i):
+        def run(updates, **layers):
+            def beside(part, pieces):
+                for k, x in enumerate(updates):
+                    if k * pieces // len(updates) == part:
+                        update(x)
+
+            stage(beside=beside, **layers)
+            for x in updates:
+                store(x).start()
+
+        load_cells(0).wait()
+        for i in range(chunk):
+            stage(
+                one=((i + 1) * rows_y, i % 2),
+                two=(i + 1) % 2 if i > 0 else None,
+                three=(i - 2, i % 2) if i > 1 else None,
+            )
+        for copy in coming + edges + load_rest(0) + load_rest(near_chunks):
+            copy.wait()
+        load_chem(0).wait()
+        load_cells(near_chunks).wait()
+        deposit(accs[0])
+
+        def step(k, carry):
+            load_cells(k).wait()
+            load_cells(near_chunks + k).wait()
+            load_chem(k).wait()
+            for copy in load_rest(k) + load_rest(near_chunks + k):
                 copy.wait()
-
-        def near_ready(i):
-            for copy in load_rest(i)[1:]:
-                copy.wait()
-
-            @pl.when(i >= spray_planes)
-            def _():
-                load_rest(i)[0].wait()
-
-        def run(i, near, **layers):
-            far_ready(i)
-            if near is not None:
-                near_ready(near)
-
-            def beside(part, pieces):
-                if near is None:
-                    update(planes + i, part, pieces)
-                elif part < pieces // 2:
-                    update(planes + i, part, pieces // 2)
-                else:
-                    update(near, part - pieces // 2, pieces - pieces // 2)
-
-            stage(beside=beside, **layers)
-            store(planes + i).start()
-            if near is not None:
-                store(near).start()
-
-        load_cells(0).wait()
-        load_cells(planes - 1).wait()
-        load_cells(planes).wait()
-        for copy in coming:
-            copy.wait()
-        for x in range(spray_planes):
-            load_rest(x)[0].wait()
-        deposit(accs[0])
-        for copy in edges:
-            copy.wait()
-
-        run(0, None, one=(rows_y, 0))
-        load_cells(1).wait()
-        run(1, None, one=(2 * rows_y, 1), two=0)
-        load_cells(2).wait()
-        run(2, None, one=(3 * rows_y, 0), two=1, three=(0, 0))
-        load_cells(3).wait()
-        run(3, 0, one=(4 * rows_y, 1), two=0, three=(1, 1))
-
-        def step(pair, carry):
-            for odd in range(2):
-                i = 2 * pair + odd
-
-                @pl.when(i < planes - 1)
-                def _():
-                    load_cells(i).wait()
-
-                run(i, i - 3, one=((i + 1) * rows_y, odd), two=1 - odd, three=(i - 2, odd))
+            for j in range(chunk):
+                i = k * chunk + j
+                far = planes + (k - 1) * more + j + 1
+                updates = [far, i - chunk + 1]
+                if j == chunk - 1:
+                    updates += [far + 1 + n for n in range(more - chunk)]
+                run(updates, one=((i + 1) * rows_y, j % 2), two=(j + 1) % 2, three=(i - 2, j % 2))
             return carry
 
-        lax.fori_loop(2, planes // 2, step, 0)
+        more = -(-(planes - 1) // (near_chunks - 1))
+        lax.fori_loop(1, near_chunks, step, 0)
         last = planes - 1
-        near_ready(last - 2)
-        stage(
+        run(
+            [planes, 0, last - 2],
             two=last % 2,
             three=(last - 1, (last - 1) % 2),
-            beside=functools.partial(update, last - 2),
-        )
-        store(last - 2).start()
-        near_ready(last - 1)
-        stage(three=(last, last % 2), beside=functools.partial(update, last - 1))
-        store(last - 1).start()
-        near_ready(last)
+        )
+        run([last - 1], three=(last, last % 2))
         update(last)
         store(last).start()
 
@@ -541,15 +532,17 @@
         pltpu.VMEM((16, hidden), bf16),
         pltpu.VMEM((16, 128), f32),
     ] + [pltpu.VMEM((hidden, rows_y * depth), bf16)] * 4
+    prepared += [pltpu.VMEM(weight.shape, weight.dtype) for weight in weights]
+    chunk = math.gcd(planes, 4)
     per_plane = 2 * rows_y * depth * hidden * (2 * comps + hidden)
     chem = pl.pallas_call(
-        functools.partial(chemistry_kernel, start=planes, planes=rest),
-        in_specs=[anywhere] + [whole] * 6,
+        functools.partial(chemistry_kernel, start=planes, planes=rest, chunk=chunk),
+        in_specs=[anywhere] * 7,
         out_specs=anywhere,
         out_shape=jax.ShapeDtypeStruct((comps, rest, rows_y, depth), f32),
         scratch_shapes=[pltpu.VMEM((comps, rest, rows_y, depth), f32)] * 2
         + prepared
-        + [sems((rest,)), sems((rest,))],
+        + [sems((rest // chunk,)), sems((rest,)), sems((len(weights),))],
         compiler_params=params,
         cost_estimate=pl.CostEstimate(
             flops=rest * per_plane,
@@ -559,10 +552,10 @@
     )(section_scores, *weights)
     tile = (comps, rows_x, rows_y, depth)
     return pl.pallas_call(
-        functools.partial(section_kernel, planes=planes, places=faces),
+        functools.partial(section_kernel, planes=planes, places=faces, chunk=chunk),
         in_specs=[anywhere] * 5
         + [pl.BlockSpec(memory_space=pl.ANY)] * (2 + len(parts))
-        + [whole] * 6,
+        + [anywhere] * 6,
         out_specs=anywhere,
         out_shape=jax.ShapeDtypeStruct(tile, f32),
         scratch_shapes=[
@@ -572,13 +565,13 @@
             pltpu.VMEM((rows_x, rows_y, depth), f32),
             pltpu.VMEM(tile, f32),
             pltpu.VMEM(tile, f32),
+            pltpu.VMEM((TILE, TILE), bf16),
         ]
         + prepared
-        + [pltpu.VMEM((TILE, TILE), bf16)]
-        + [sems((rows_x,))] * 4
-        + [sems((rest,)), sems((2,)), sems((rows_x,))]
+        + [sems((rows_x // chunk,))] * 4
+        + [sems((rest // chunk,)), sems((2,)), sems((rows_x,))]
         + [pltpu.VMEM(part.shape, f32) for part in parts]
-        + [sems((len(parts),))],
+        + [sems((len(parts),)), sems((len(weights),))],
         compiler_params=params,
         cost_estimate=pl.CostEstimate(
             flops=planes * per_plane,

time: 59.7 us -> 54 us (0.905)
  Pallas kernels: 44.5 us -> 38.6 us
    pallas_call x1, Pallas kernels: 23.8 us -> 19.7 us  [shards(): pl.pallas_call(functools.partial(section_kernel, planes=planes, places=fa...]
    pallas_call x1, Pallas kernels: 16.9 us -> 15.1 us  [shards(): pl.pallas_call(functools.partial(chemistry_kernel, start=planes, planes=r...]
where the time goes in v3:
time: 54 us; the launch traced here: 53.7 us
  Pallas kernels  38.6 us (71%)
  starting transfers between devices  10 us (19%)
  local copies, waits for them, and re-layouts  3.23 us (6%)
  matrix products  1.5 us (3%)
    pallas_call x1, Pallas kernels, shards(): pl.pallas_call(functools.partial(section_kernel, planes=planes, places=fa...  19.7 us
    pallas_call x1, Pallas kernels, shards(): pl.pallas_call(functools.partial(chemistry_kernel, start=planes, planes=r...  15.1 us
    pallas_call x1, Pallas kernels, shards(): pl.pallas_call(functools.partial(faces_kernel, shifts=shifts), in_specs=[...  3.83 us
    ppermute x1, starting transfers between devices, shards(): from_low_x = lax.ppermute(high_x, 'gx', forward)  3.43 us
    ppermute x1, starting transfers between devices, shards(): from_high_x = lax.ppermute(low_x, 'gx', backward)  3.31 us
    ppermute x3, starting transfers between devices, shards(): lax.ppermute(send, 'gy', [(i, (i + shift) % tiles_y) for i in range(tiles...  3.3 us
    unnamed x12, local copies, waits for them, and re-layouts  2.55 us
    dot_general x1, matrix products, shards(): jnp.einsum('ks,psc->kpc', loadings, parcel_species, preferred_element_typ...  1.5 us
  transfers between devices with their start and end apart: 5, of which 0 were waited for; matrix products, arithmetic and copies ran while one was open for 0% of the time, Pallas kernels for 28%

profile of v3, /device:TPU:8, one launch (start us, length us, event | category | flops | bytes accessed | tf_op | source)
XLA Modules:
  0.0 53.7 jit_solution(9910765451717468854)
XLA Ops:
  0.0 0.0 copy-start
  0.0 1.7 %copy-done = bf16[32,300,128]{2,0,1:T(8,128)(2,1)S(1)} copy-done((bf16[32,300,128]{2,0,1:T(8,128)(2,1)S(1)}, bf16[32,300,128]{2,0,1:T(8,128)(2,1)}, u32[]{:S(2)}) %copy-start) | copy-done | bytes 2457624
  1.7 1.5 %fusion = bf16[12,32,128]{2,0,1:T(8,128)(2,1)S(1)} fusion(bf16[32,300,128]{2,0,1:T(8,128)(2,1)S(1)} %copy-done, bf16[12,300]{1,0:T(8,128)(2,1)} %param.24), kind=kOutput, calls=%fused_computation | convolution fusion | flops 29491200 | bytes 2563104 | tf_op jit(solution)/shard_map/ks,psc->kpc/dot_general | solution.py:495
  3.2 0.7 %copy.20.projected = bf16[12,32,128]{2,1,0:T(8,128)(2,1)} copy(bf16[12,32,128]{2,0,1:T(8,128)(2,1)S(1)} %fusion) | data formatting | bytes 196608 | tf_op jit(solution)/shard_map/ks,psc->kpc/dot_general | solution.py:495
  3.9 3.8 %shard_map.137 = (f32[12,16,128]{2,1,0:T(8,128)}, f32[12,16,128]{2,1,0:T(8,128)}, f32[13,16,128]{2,1,0:T(8,128)}, f32[13,48,128]{2,1,0:T(8,128)}, f32[13,48,128]{2,1,0:T(8,128)}, /*index=5*/f32[13,16,128]{2,1,0:T(8,128)}) custom-call(s32[1,32]{1,0:T(1,128)} %bitcast.9, s32[1,32]{1,0:T(1,128)} %bitcast.10, bf16[12,32,128]{2,1,0:T(8,128)(2,1)} %copy.20.projected, ...), custom_call_target="tpu_custom_call" | custom-call | tf_op jit(solution)/shard_map/pallas_call | solution.py:501
  7.7 3.4 %collective-permute-start = (f32[12,16,128]{2,1,0:T(8,128)}, f32[12,16,128]{2,1,0:T(8,128)S(1)}, u32[]{:S(2)}, u32[]{:S(2)}) collective-permute-start(f32[12,16,128]{2,1,0:T(8,128)} %get-tuple-element.11), channel_id=1, source_target_pairs={{0,4},{4,8},{8,12},{12,16},{16,20},{20,24},{24,28},{1,5},{5,9},{9,... | collective-permute-start | bytes 294920 | tf_op jit(solution)/shard_map/ppermute | solution.py:514
  11.1 3.3 %collective-permute-start.1 = (f32[12,16,128]{2,1,0:T(8,128)}, f32[12,16,128]{2,1,0:T(8,128)S(1)}, u32[]{:S(2)}, u32[]{:S(2)}) collective-permute-start(f32[12,16,128]{2,1,0:T(8,128)} %get-tuple-element.12), channel_id=1, source_target_pairs={{4,0},{8,4},{12,8},{16,12},{20,16},{24,20},{28,24},{5,1},{9,5},{13... | collective-permute-start | bytes 294920 | tf_op jit(solution)/shard_map/ppermute | solution.py:515
  14.5 1.6 %collective-permute-start.4 = (f32[13,16,128]{2,1,0:T(8,128)}, f32[13,16,128]{2,1,0:T(8,128)S(1)}, u32[]{:S(2)}, u32[]{:S(2)}) collective-permute-start(f32[13,16,128]{2,1,0:T(8,128)} %get-tuple-element.16), channel_id=1, source_target_pairs={{0,2},{1,3},{2,0},{3,1},{4,6},{5,7},{6,4},{7,5},{8,10},{9,11},{10,... | collective-permute-start | bytes 319496 | tf_op jit(solution)/shard_map/ppermute | solution.py:517
  16.0 0.0 collective-permute-start.2
  16.0 1.7 %collective-permute-start.3 = (f32[13,48,128]{2,1,0:T(8,128)}, f32[13,48,128]{2,1,0:T(8,128)S(1)}, u32[]{:S(2)}, u32[]{:S(2)}) collective-permute-start(f32[13,48,128]{2,1,0:T(8,128)} %get-tuple-element.15), channel_id=1, source_target_pairs={{0,3},{1,0},{2,1},{3,2},{4,7},{5,4},{6,5},{7,6},{8,11},{9,8},{10,9... | collective-permute-start | bytes 958472 | tf_op jit(solution)/shard_map/ppermute | solution.py:517
  17.8 15.1 %shard_map.136.chem_in = f32[12,16,16,128]{3,2,1,0:T(8,128)} custom-call(f32[12,32,16,128]{3,2,1,0:T(8,128)} %section.5, bf16[12,256]{1,0:T(8,128)(2,1)} %bitcast.11, f32[1,256]{1,0:T(1,128)} %bitcast.13, bf16[256,256]{1,0:T(8,128)(2,1)} %refs_6_.1, f32[1,256]{1,0:T(1,128)} %bitcast.15, bf16[12,256]{1,0:T(8,128)(2,1)} %refs_8_.1, f32[1,12]{1,0:T(1,128)} %bitcast.17), custom_call_target="tpu_custom_call" | custom-call | flops 4697620480 | bytes 3145728 | tf_op jit(solution)/shard_map/pallas_call | solution.py:538
  32.9 0.0 collective-permute-done.from_low_x
  32.9 0.0 copy-start.4
  32.9 0.0 collective-permute-done.1.from_high_x
  32.9 0.0 copy-start.5
  32.9 0.0 collective-permute-done.4.refs_3_
  33.0 0.0 copy-start.3
  33.0 0.0 collective-permute-done.2.refs_1_
  33.0 0.0 copy-start.1
  33.0 0.0 collective-permute-done.3.refs_2_
  33.0 0.0 copy-start.2
  33.0 0.5 %copy-done.4 = f32[12,16,128]{2,1,0:T(8,128)} copy-done((f32[12,16,128]{2,1,0:T(8,128)}, f32[12,16,128]{2,1,0:T(8,128)S(1)}, u32[]{:S(2)}) %copy-start.4) | copy-done | bytes 98328
  33.5 0.0 copy-done.5
  33.6 0.0 copy-done.3
  33.6 0.1 copy-done.1
  33.8 0.1 copy-done.2
  33.9 19.7 %shard_map.138 = f32[12,32,16,128]{3,2,1,0:T(8,128)} custom-call(f32[12,32,16,128]{3,2,1,0:T(8,128)} %section.5, f32[12,32,16,128]{3,2,1,0:T(8,128)} %base.1, f32[3,32,16,128]{3,2,1,0:T(8,128)} %velocity.1, f32[32,16,128]{2,1,0:T(8,128)} %diffusivity.1, f32[12,16,16,128]{3,2,1,0:T(8,128)} %shard_map.136.chem_in, f32[12,16,128]{2,1,0:T(8,128)} %copy-done.4, ...), custom_call_target="tpu_custom_call" | custom-call | flops 4697620480 | bytes 12582912 | tf_op jit(solution)/shard_map/pallas_call | solution.py:554
Async XLA Ops:
  0.0 1.7 %copy-start = (bf16[32,300,128]{2,0,1:T(8,128)(2,1)S(1)}, bf16[32,300,128]{2,0,1:T(8,128)(2,1)}, u32[]{:S(2)}) copy-start(bf16[32,300,128]{2,0,1:T(8,128)(2,1)} %param.25) | copy-start | bytes 7372804
  7.7 25.2 %collective-permute-start = (f32[12,16,128]{2,1,0:T(8,128)}, f32[12,16,128]{2,1,0:T(8,128)S(1)}, u32[]{:S(2)}, u32[]{:S(2)}) collective-permute-start(f32[12,16,128]{2,1,0:T(8,128)} %get-tuple-element.11), channel_id=1, source_target_pairs={{0,4},{4,8},{8,12},{12,16},{16,20},{20,24},{24,28},{1,5},{5,9},{9,... | collective-permute-start | bytes 294920 | tf_op jit(solution)/shard_map/ppermute | solution.py:514
  11.1 21.8 %collective-permute-start.1 = (f32[12,16,128]{2,1,0:T(8,128)}, f32[12,16,128]{2,1,0:T(8,128)S(1)}, u32[]{:S(2)}, u32[]{:S(2)}) collective-permute-start(f32[12,16,128]{2,1,0:T(8,128)} %get-tuple-element.12), channel_id=1, source_target_pairs={{4,0},{8,4},{12,8},{16,12},{20,16},{24,20},{28,24},{5,1},{9,5},{13... | collective-permute-start | bytes 294920 | tf_op jit(solution)/shard_map/ppermute | solution.py:515
  14.5 18.5 %collective-permute-start.4 = (f32[13,16,128]{2,1,0:T(8,128)}, f32[13,16,128]{2,1,0:T(8,128)S(1)}, u32[]{:S(2)}, u32[]{:S(2)}) collective-permute-start(f32[13,16,128]{2,1,0:T(8,128)} %get-tuple-element.16), channel_id=1, source_target_pairs={{0,2},{1,3},{2,0},{3,1},{4,6},{5,7},{6,4},{7,5},{8,10},{9,11},{10,... | collective-permute-start | bytes 319496 | tf_op jit(solution)/shard_map/ppermute | solution.py:517
  16.0 16.9 %collective-permute-start.2 = (f32[13,48,128]{2,1,0:T(8,128)}, f32[13,48,128]{2,1,0:T(8,128)S(1)}, u32[]{:S(2)}, u32[]{:S(2)}) collective-permute-start(f32[13,48,128]{2,1,0:T(8,128)} %get-tuple-element.14), channel_id=1, source_target_pairs={{0,1},{1,2},{2,3},{3,0},{4,5},{5,6},{6,7},{7,4},{8,9},{9,10},{10,1... | collective-permute-start | bytes 958472 | tf_op jit(solution)/shard_map/ppermute | solution.py:517
  16.0 17.0 %collective-permute-start.3 = (f32[13,48,128]{2,1,0:T(8,128)}, f32[13,48,128]{2,1,0:T(8,128)S(1)}, u32[]{:S(2)}, u32[]{:S(2)}) collective-permute-start(f32[13,48,128]{2,1,0:T(8,128)} %get-tuple-element.15), channel_id=1, source_target_pairs={{0,3},{1,0},{2,1},{3,2},{4,7},{5,4},{6,5},{7,6},{8,11},{9,8},{10,9... | collective-permute-start | bytes 958472 | tf_op jit(solution)/shard_map/ppermute | solution.py:517
  32.9 0.6 %copy-start.4 = (f32[12,16,128]{2,1,0:T(8,128)}, f32[12,16,128]{2,1,0:T(8,128)S(1)}, u32[]{:S(2)}) copy-start(f32[12,16,128]{2,1,0:T(8,128)S(1)} %collective-permute-done.from_low_x) | copy-start | bytes 294916
  32.9 0.7 %copy-start.5 = (f32[12,16,128]{2,1,0:T(8,128)}, f32[12,16,128]{2,1,0:T(8,128)S(1)}, u32[]{:S(2)}) copy-start(f32[12,16,128]{2,1,0:T(8,128)S(1)} %collective-permute-done.1.from_high_x) | copy-start | bytes 294916
  33.0 0.7 %copy-start.3 = (f32[13,16,128]{2,1,0:T(8,128)}, f32[13,16,128]{2,1,0:T(8,128)S(1)}, u32[]{:S(2)}) copy-start(f32[13,16,128]{2,1,0:T(8,128)S(1)} %collective-permute-done.4.refs_3_) | copy-start | bytes 319492
  33.0 0.8 %copy-start.1 = (f32[13,48,128]{2,1,0:T(8,128)}, f32[13,48,128]{2,1,0:T(8,128)S(1)}, u32[]{:S(2)}) copy-start(f32[13,48,128]{2,1,0:T(8,128)S(1)} %collective-permute-done.2.refs_1_) | copy-start | bytes 958468
  33.0 0.9 %copy-start.2 = (f32[13,48,128]{2,1,0:T(8,128)}, f32[13,48,128]{2,1,0:T(8,128)S(1)}, u32[]{:S(2)}) copy-start(f32[13,48,128]{2,1,0:T(8,128)S(1)} %collective-permute-done.3.refs_2_) | copy-start | bytes 958468

commit v4 on v3

--- a/solution.py
+++ b/solution.py
@@ -158,9 +158,9 @@
             load_sem.at[k],
         )
 
-    def store(i):
+    def store(i, some):
         return pltpu.make_async_copy(
-            held.at[:, pl.ds(i, 1)], out.at[:, pl.ds(i, 1)], store_sem.at[i]
+            held.at[:, pl.ds(i, some)], out.at[:, pl.ds(i, some)], store_sem.at[i]
         )
 
     load(0).start()
@@ -184,7 +184,6 @@
         )
         def run(i, odd):
             stage(one=(i * rows_y, odd), two=1 - odd, three=(i - 2, odd))
-            store(i - 2).start()
 
         load(0).wait()
         stage(one=(0, 0))
@@ -196,18 +195,21 @@
             load(k).wait()
             for j in range(chunk):
                 run(k * chunk + j, j % 2)
+            store((k - 1) * chunk, chunk).start()
             return carry
 
         lax.fori_loop(1, planes // chunk, step, 0)
         last = planes - 1
+        store(planes - chunk, chunk - 2).start()
         stage(two=last % 2, three=(last - 1, (last - 1) % 2))
-        store(last - 1).start()
         stage(three=(last, last % 2))
-        store(last).start()
+        store(last - 1, 2).start()
 
     accumulators(body)
-    for i in range(planes):
-        store(i).wait()
+    for k in range(1, planes // chunk):
+        store((k - 1) * chunk, chunk).wait()
+    store(planes - chunk, chunk - 2).wait()
+    store(planes - 2, 2).wait()
 
 
 def section_kernel(section, base, velocity, diffusivity, chem_in, from_low_x, from_high_x, *refs, planes, places, chunk):
@@ -252,10 +254,18 @@
             chem_sem.at[k],
         )
 
-    def store(x):
+    def store(x, some=1):
         return pltpu.make_async_copy(
-            out_s.at[:, pl.ds(x, 1)], out.at[:, pl.ds(x, 1)], store_sem.at[x]
-        )
+            out_s.at[:, pl.ds(x, some)], out.at[:, pl.ds(x, some)], store_sem.at[x]
+        )
+
+    more = -(-(planes - 1) // (near_chunks - 1))
+
+    def loop_stores(k):
+        return [
+            store((k - 1) * chunk + 1, chunk),
+            store(planes + (k - 1) * more + 1, more),
+        ]
 
     edges = [
         pltpu.make_async_copy(from_low_x, cells.at[:, 0], edge_sem.at[0]),
@@ -357,8 +367,6 @@
                         update(x)
 
             stage(beside=beside, **layers)
-            for x in updates:
-                store(x).start()
 
         load_cells(0).wait()
         for i in range(chunk):
@@ -386,9 +394,10 @@
                 if j == chunk - 1:
                     updates += [far + 1 + n for n in range(more - chunk)]
                 run(updates, one=((i + 1) * rows_y, j % 2), two=(j + 1) % 2, three=(i - 2, j % 2))
+            for copy in loop_stores(k):
+                copy.start()
             return carry
 
-        more = -(-(planes - 1) // (near_chunks - 1))
         lax.fori_loop(1, near_chunks, step, 0)
         last = planes - 1
         run(
@@ -397,11 +406,16 @@
             three=(last - 1, (last - 1) % 2),
         )
         run([last - 1], three=(last, last % 2))
+        for x in (planes, 0, last - 2, last - 1):
+            store(x).start()
         update(last)
         store(last).start()
 
     accumulators(body)
-    for x in range(all_planes):
+    for k in range(1, near_chunks):
+        for copy in loop_stores(k):
+            copy.wait()
+    for x in (planes, 0, planes - 3, planes - 2, planes - 1):
         store(x).wait()
 
 
@@ -490,7 +504,7 @@
     whole = pl.BlockSpec(memory_space=pltpu.VMEM)
     anywhere = pl.BlockSpec(memory_space=pltpu.HBM)
     sems = pltpu.SemaphoreType.DMA
-    params = pltpu.CompilerParams(vmem_limit_bytes=60 * 2**20)
+    params = pltpu.CompilerParams(vmem_limit_bytes=32 * 2**20)
 
     projected = jnp.einsum(
         "ks,psc->kpc", loadings, parcel_species, preferred_element_type=f32

time: 54 us -> 48.5 us (0.90)
  Pallas kernels: 38.6 us -> 32.7 us
    pallas_call x1, Pallas kernels: 3.83 us -> 0.69 us  [shards(): pl.pallas_call(functools.partial(faces_kernel, shifts=shifts), in_specs=[...]
    pallas_call x1, Pallas kernels: 15.1 us -> 13.6 us  [shards(): pl.pallas_call(functools.partial(chemistry_kernel, start=planes, planes=r...]
    pallas_call x1, Pallas kernels: 19.7 us -> 18.4 us  [shards(): pl.pallas_call(functools.partial(section_kernel, planes=planes, places=fa...]
    unnamed x12 -> x26, local copies, waits for them, and re-layouts: 2.55 us -> 3.56 us
    dot_general x1, local copies, waits for them, and re-layouts: 0.68 us -> 0.03 us  [shards(): jnp.einsum('ks,psc->kpc', loadings, parcel_species, preferred_element_typ...]
where the time goes in v4:
time: 48.5 us; the launch traced here: 48.2 us
  Pallas kernels  32.7 us (67%)
  starting transfers between devices  10 us (21%)
  local copies, waits for them, and re-layouts  3.59 us (7%)
  matrix products  1.5 us (3%)
    pallas_call x1, Pallas kernels, shards(): pl.pallas_call(functools.partial(section_kernel, planes=planes, places=fa...  18.4 us
    pallas_call x1, Pallas kernels, shards(): pl.pallas_call(functools.partial(chemistry_kernel, start=planes, planes=r...  13.6 us
    unnamed x26, local copies, waits for them, and re-layouts  3.56 us
    ppermute x1, starting transfers between devices, shards(): from_low_x = lax.ppermute(high_x, 'gx', forward)  3.43 us
    ppermute x1, starting transfers between devices, shards(): from_high_x = lax.ppermute(low_x, 'gx', backward)  3.31 us
    ppermute x3, starting transfers between devices, shards(): lax.ppermute(send, 'gy', [(i, (i + shift) % tiles_y) for i in range(tiles...  3.3 us
    dot_general x1, matrix products, shards(): jnp.einsum('ks,psc->kpc', loadings, parcel_species, preferred_element_typ...  1.5 us
  transfers between devices with their start and end apart: 5, of which 0 were waited for; matrix products, arithmetic and copies ran while one was open for 0% of the time, Pallas kernels for 28%

profile of v4, /device:TPU:8, one launch (start us, length us, event | category | flops | bytes accessed | tf_op | source)
XLA Modules:
  0.0 48.2 jit_solution(6319998396557250296)
XLA Ops:
  0.0 0.0 copy-start
  0.0 0.0 copy-start.3
  0.0 0.0 copy-start.2
  0.0 0.0 copy-start.9
  0.0 0.0 copy-start.7
  0.0 0.0 copy-start.12
  0.0 0.0 copy-start.11
  0.1 0.0 copy-start.10
  0.1 0.0 copy-start.8
  0.1 1.6 %copy-done = bf16[32,300,128]{2,0,1:T(8,128)(2,1)S(1)} copy-done((bf16[32,300,128]{2,0,1:T(8,128)(2,1)S(1)}, bf16[32,300,128]{2,0,1:T(8,128)(2,1)}, u32[]{:S(2)}) %copy-start) | copy-done | bytes 2457624
  1.7 1.5 %fusion = bf16[12,32,128]{2,0,1:T(8,128)(2,1)S(1)} fusion(bf16[32,300,128]{2,0,1:T(8,128)(2,1)S(1)} %copy-done, bf16[12,300]{1,0:T(8,128)(2,1)} %param.24), kind=kOutput, calls=%fused_computation | convolution fusion | flops 29491200 | bytes 2563104 | tf_op jit(solution)/shard_map/ks,psc->kpc/dot_general | solution.py:509
  3.2 0.0 copy-done.3
  3.2 0.0 copy-done.2
  3.2 0.0 copy-start.1
  3.3 1.9 %copy-done.1 = f32[12,32,16,128]{3,2,1,0:T(8,128)S(1)} copy-done((f32[12,32,16,128]{3,2,1,0:T(8,128)S(1)}, f32[12,32,16,128]{3,2,1,0:T(8,128)}, u32[]{:S(2)}) %copy-start.1) | copy-done | bytes 3145752
  5.1 0.7 %shard_map.137 = (f32[12,16,128]{2,1,0:T(8,128)S(1)}, f32[12,16,128]{2,1,0:T(8,128)S(1)}, f32[13,16,128]{2,1,0:T(8,128)S(1)}, f32[13,48,128]{2,1,0:T(8,128)S(1)}...) custom-call(s32[1,32]{1,0:T(1,128)S(1)} %bitcast.9, s32[1,32]{1,0:T(1,128)S(1)} %bitcast.10, ...), custom_call_target="tpu_custom_call" | custom-call | tf_op jit(solution)/shard_map/pallas_call | solution.py:515
  5.8 3.4 %collective-permute-start = (f32[12,16,128]{2,1,0:T(8,128)S(1)}, f32[12,16,128]{2,1,0:T(8,128)S(1)}, u32[]{:S(2)}, u32[]{:S(2)}) collective-permute-start(f32[12,16,128]{2,1,0:T(8,128)S(1)} %get-tuple-element.11), channel_id=1, source_target_pairs={{0,4},{4,8},{8,12},{12,16},{16,20},{20,24},{24,28},{1,5},{5,9},{9,... | collective-permute-start | bytes 294920 | tf_op jit(solution)/shard_map/ppermute | solution.py:528
  9.3 3.3 %collective-permute-start.1 = (f32[12,16,128]{2,1,0:T(8,128)S(1)}, f32[12,16,128]{2,1,0:T(8,128)S(1)}, u32[]{:S(2)}, u32[]{:S(2)}) collective-permute-start(f32[12,16,128]{2,1,0:T(8,128)S(1)} %get-tuple-element.12), channel_id=1, source_target_pairs={{4,0},{8,4},{12,8},{16,12},{20,16},{24,20},{28,24},{5,1},{9,5},{13... | collective-permute-start | bytes 294920 | tf_op jit(solution)/shard_map/ppermute | solution.py:529
  12.6 1.6 %collective-permute-start.4 = (f32[13,16,128]{2,1,0:T(8,128)S(1)}, f32[13,16,128]{2,1,0:T(8,128)S(1)}, u32[]{:S(2)}, u32[]{:S(2)}) collective-permute-start(f32[13,16,128]{2,1,0:T(8,128)S(1)} %get-tuple-element.16), channel_id=1, source_target_pairs={{0,2},{1,3},{2,0},{3,1},{4,6},{5,7},{6,4},{7,5},{8,10},{9,11},{10,... | collective-permute-start | bytes 319496 | tf_op jit(solution)/shard_map/ppermute | solution.py:531
  14.2 0.0 collective-permute-start.2
  14.2 1.7 %collective-permute-start.3 = (f32[13,48,128]{2,1,0:T(8,128)S(1)}, f32[13,48,128]{2,1,0:T(8,128)S(1)}, u32[]{:S(2)}, u32[]{:S(2)}) collective-permute-start(f32[13,48,128]{2,1,0:T(8,128)S(1)} %get-tuple-element.15), channel_id=1, source_target_pairs={{0,3},{1,0},{2,1},{3,2},{4,7},{5,4},{6,5},{7,6},{8,11},{9,8},{10,9... | collective-permute-start | bytes 958472 | tf_op jit(solution)/shard_map/ppermute | solution.py:531
  15.9 0.0 copy-done.9
  15.9 0.0 copy-done.7
  15.9 0.0 copy-done.12
  15.9 0.0 copy-done.11
  15.9 0.0 copy-done.10
  15.9 0.0 copy-done.8
  15.9 0.0 copy-start.4
  16.0 0.0 copy-start.5
  16.0 0.0 copy-start.6
  16.0 13.6 %shard_map.136.chem_in = f32[12,16,16,128]{3,2,1,0:T(8,128)S(1)} custom-call(f32[12,32,16,128]{3,2,1,0:T(8,128)S(1)} %copy-done.1, bf16[12,256]{1,0:T(8,128)(2,1)S(1)} %bitcast.11, f32[1,256]{1,0:T(1,128)S(1)} %bitcast.13, bf16[256,256]{1,0:T(8,128)(2,1)S(1)} %copy-done.7, f32[1,256]{1,0:T(1,128)S(1)} %bitcast.15, bf16[12,256]{1,0:T(8,128)(2,1)S(1)} %copy-done.9, ...), custom_call_target="tpu_custom_call" | custom-call | flops 4697620480 | bytes 3145728 | tf_op jit(solution)/shard_map/pallas_call | solution.py:552
  29.6 0.0 collective-permute-done.from_low_x
  29.6 0.0 collective-permute-done.1.from_high_x
  29.6 0.0 collective-permute-done.4.refs_3_
  29.6 0.0 collective-permute-done.2.refs_1_
  29.6 0.0 collective-permute-done.3.refs_2_
  29.6 0.0 copy-done.4
  29.7 0.0 copy-done.5
  29.7 0.0 copy-done.6
  29.7 18.4 %shard_map.138 = f32[12,32,16,128]{3,2,1,0:T(8,128)} custom-call(f32[12,32,16,128]{3,2,1,0:T(8,128)S(1)} %copy-done.1, f32[12,32,16,128]{3,2,1,0:T(8,128)S(1)} %copy-done.4, f32[3,32,16,128]{3,2,1,0:T(8,128)S(1)} %copy-done.5, f32[32,16,128]{2,1,0:T(8,128)S(1)} %copy-done.6, f32[12,16,16,128]{3,2,1,0:T(8,128)S(1)} %shard_map.136.chem_in, ...), custom_call_target="tpu_custom_call" | custom-call | flops 4697620480 | bytes 12582912 | tf_op jit(solution)/shard_map/pallas_call | solution.py:568
  (1 shorter events, 0.0 us)
Async XLA Ops:
  0.0 1.7 %copy-start = (bf16[32,300,128]{2,0,1:T(8,128)(2,1)S(1)}, bf16[32,300,128]{2,0,1:T(8,128)(2,1)}, u32[]{:S(2)}) copy-start(bf16[32,300,128]{2,0,1:T(8,128)(2,1)} %param.25) | copy-start | bytes 7372804
  0.0 3.2 %copy-start.3 = (s32[32]{0:T(128)S(1)}, s32[32]{0:T(128)}, u32[]{:S(2)}) copy-start(s32[32]{0:T(128)} %param.27) | copy-start | bytes 388
  0.0 3.2 %copy-start.2 = (s32[32,1]{0,1:T(1,128)S(1)}, s32[32,1]{0,1:T(1,128)}, u32[]{:S(2)}) copy-start(s32[32,1]{0,1:T(1,128)} %param.26) | copy-start | bytes 388
  0.0 15.9 %copy-start.9 = (bf16[12,256]{1,0:T(8,128)(2,1)S(1)}, bf16[12,256]{1,0:T(8,128)(2,1)}, u32[]{:S(2)}) copy-start(bf16[12,256]{1,0:T(8,128)(2,1)} %refs_8_.1) | copy-start | bytes 18436
  0.0 15.9 %copy-start.7 = (bf16[256,256]{1,0:T(8,128)(2,1)S(1)}, bf16[256,256]{1,0:T(8,128)(2,1)}, u32[]{:S(2)}) copy-start(bf16[256,256]{1,0:T(8,128)(2,1)} %refs_6_.1) | copy-start | bytes 393220
  0.0 15.9 %copy-start.12 = (f32[12]{0:T(128)S(1)}, f32[12]{0:T(128)}, u32[]{:S(2)}) copy-start(f32[12]{0:T(128)} %param.23) | copy-start | bytes 148
  0.0 15.9 %copy-start.11 = (f32[256]{0:T(256)S(1)}, f32[256]{0:T(256)}, u32[]{:S(2)}) copy-start(f32[256]{0:T(256)} %param.21) | copy-start | bytes 3076
  0.1 15.9 %copy-start.10 = (f32[256]{0:T(256)S(1)}, f32[256]{0:T(256)}, u32[]{:S(2)}) copy-start(f32[256]{0:T(256)} %param.19) | copy-start | bytes 3076
  0.1 15.9 %copy-start.8 = (bf16[256,12]{0,1:T(8,128)(2,1)S(1)}, bf16[256,12]{0,1:T(8,128)(2,1)}, u32[]{:S(2)}) copy-start(bf16[256,12]{0,1:T(8,128)(2,1)} %param.18) | copy-start | bytes 18436
  3.2 1.9 %copy-start.1 = (f32[12,32,16,128]{3,2,1,0:T(8,128)S(1)}, f32[12,32,16,128]{3,2,1,0:T(8,128)}, u32[]{:S(2)}) copy-start(f32[12,32,16,128]{3,2,1,0:T(8,128)} %section.5) | copy-start | bytes 9437188
  5.8 23.7 %collective-permute-start = (f32[12,16,128]{2,1,0:T(8,128)S(1)}, f32[12,16,128]{2,1,0:T(8,128)S(1)}, u32[]{:S(2)}, u32[]{:S(2)}) collective-permute-start(f32[12,16,128]{2,1,0:T(8,128)S(1)} %get-tuple-element.11), channel_id=1, source_target_pairs={{0,4},{4,8},{8,12},{12,16},{16,20},{20,24},{24,28},{1,5},{5,9},{9,... | collective-permute-start | bytes 294920 | tf_op jit(solution)/shard_map/ppermute | solution.py:528
  9.3 20.3 %collective-permute-start.1 = (f32[12,16,128]{2,1,0:T(8,128)S(1)}, f32[12,16,128]{2,1,0:T(8,128)S(1)}, u32[]{:S(2)}, u32[]{:S(2)}) collective-permute-start(f32[12,16,128]{2,1,0:T(8,128)S(1)} %get-tuple-element.12), channel_id=1, source_target_pairs={{4,0},{8,4},{12,8},{16,12},{20,16},{24,20},{28,24},{5,1},{9,5},{13... | collective-permute-start | bytes 294920 | tf_op jit(solution)/shard_map/ppermute | solution.py:529
  12.6 17.0 %collective-permute-start.4 = (f32[13,16,128]{2,1,0:T(8,128)S(1)}, f32[13,16,128]{2,1,0:T(8,128)S(1)}, u32[]{:S(2)}, u32[]{:S(2)}) collective-permute-start(f32[13,16,128]{2,1,0:T(8,128)S(1)} %get-tuple-element.16), channel_id=1, source_target_pairs={{0,2},{1,3},{2,0},{3,1},{4,6},{5,7},{6,4},{7,5},{8,10},{9,11},{10,... | collective-permute-start | bytes 319496 | tf_op jit(solution)/shard_map/ppermute | solution.py:531
  14.2 15.5 %collective-permute-start.2 = (f32[13,48,128]{2,1,0:T(8,128)S(1)}, f32[13,48,128]{2,1,0:T(8,128)S(1)}, u32[]{:S(2)}, u32[]{:S(2)}) collective-permute-start(f32[13,48,128]{2,1,0:T(8,128)S(1)} %get-tuple-element.14), channel_id=1, source_target_pairs={{0,1},{1,2},{2,3},{3,0},{4,5},{5,6},{6,7},{7,4},{8,9},{9,10},{10,1... | collective-permute-start | bytes 958472 | tf_op jit(solution)/shard_map/ppermute | solution.py:531
  14.2 15.5 %collective-permute-start.3 = (f32[13,48,128]{2,1,0:T(8,128)S(1)}, f32[13,48,128]{2,1,0:T(8,128)S(1)}, u32[]{:S(2)}, u32[]{:S(2)}) collective-permute-start(f32[13,48,128]{2,1,0:T(8,128)S(1)} %get-tuple-element.15), channel_id=1, source_target_pairs={{0,3},{1,0},{2,1},{3,2},{4,7},{5,4},{6,5},{7,6},{8,11},{9,8},{10,9... | collective-permute-start | bytes 958472 | tf_op jit(solution)/shard_map/ppermute | solution.py:531
  15.9 13.7 %copy-start.4 = (f32[12,32,16,128]{3,2,1,0:T(8,128)S(1)}, f32[12,32,16,128]{3,2,1,0:T(8,128)}, u32[]{:S(2)}) copy-start(f32[12,32,16,128]{3,2,1,0:T(8,128)} %base.1) | copy-start | bytes 9437188
  16.0 13.7 %copy-start.5 = (f32[3,32,16,128]{3,2,1,0:T(8,128)S(1)}, f32[3,32,16,128]{3,2,1,0:T(8,128)}, u32[]{:S(2)}) copy-start(f32[3,32,16,128]{3,2,1,0:T(8,128)} %velocity.1) | copy-start | bytes 2359300
  16.0 13.7 %copy-start.6 = (f32[32,16,128]{2,1,0:T(8,128)S(1)}, f32[32,16,128]{2,1,0:T(8,128)}, u32[]{:S(2)}) copy-start(f32[32,16,128]{2,1,0:T(8,128)} %diffusivity.1) | copy-start | bytes 786436

commit v5 on v4

--- a/solution.py
+++ b/solution.py
@@ -567,8 +567,8 @@
     tile = (comps, rows_x, rows_y, depth)
     return pl.pallas_call(
         functools.partial(section_kernel, planes=planes, places=faces, chunk=chunk),
-        in_specs=[anywhere] * 5
-        + [pl.BlockSpec(memory_space=pl.ANY)] * (2 + len(parts))
+        in_specs=[anywhere]
+        + [pl.BlockSpec(memory_space=pl.ANY)] * (6 + len(parts))
         + [anywhere] * 6,
         out_specs=anywhere,
         out_shape=jax.ShapeDtypeStruct(tile, f32),

time: 48.5 us -> 48.5 us (level)
  no operation moved by 1% of the time
where the time goes in v5:
time: 48.5 us; the launch traced here: 48.2 us
  Pallas kernels  32.7 us (67%)
  starting transfers between devices  10 us (21%)
  local copies, waits for them, and re-layouts  3.59 us (7%)
  matrix products  1.5 us (3%)
    pallas_call x1, Pallas kernels, shards(): pl.pallas_call(functools.partial(section_kernel, planes=planes, places=fa...  18.4 us
    pallas_call x1, Pallas kernels, shards(): pl.pallas_call(functools.partial(chemistry_kernel, start=planes, planes=r...  13.6 us
    unnamed x26, local copies, waits for them, and re-layouts  3.56 us
    ppermute x1, starting transfers between devices, shards(): from_low_x = lax.ppermute(high_x, 'gx', forward)  3.43 us
    ppermute x1, starting transfers between devices, shards(): from_high_x = lax.ppermute(low_x, 'gx', backward)  3.31 us
    ppermute x3, starting transfers between devices, shards(): lax.ppermute(send, 'gy', [(i, (i + shift) % tiles_y) for i in range(tiles...  3.3 us
    dot_general x1, matrix products, shards(): jnp.einsum('ks,psc->kpc', loadings, parcel_species, preferred_element_typ...  1.5 us
  transfers between devices with their start and end apart: 5, of which 0 were waited for; matrix products, arithmetic and copies ran while one was open for 0% of the time, Pallas kernels for 28%

profile of v5, /device:TPU:8, one launch (start us, length us, event | category | flops | bytes accessed | tf_op | source)
XLA Modules:
  0.0 48.2 jit_solution(6319998396557250296)
XLA Ops:
  0.0 0.0 copy-start
  0.0 0.0 copy-start.3
  0.0 0.0 copy-start.2
  0.0 0.0 copy-start.9
  0.0 0.0 copy-start.7
  0.0 0.0 copy-start.12
  0.0 0.0 copy-start.11
  0.1 0.0 copy-start.10
  0.1 0.0 copy-start.8
  0.1 1.6 %copy-done = bf16[32,300,128]{2,0,1:T(8,128)(2,1)S(1)} copy-done((bf16[32,300,128]{2,0,1:T(8,128)(2,1)S(1)}, bf16[32,300,128]{2,0,1:T(8,128)(2,1)}, u32[]{:S(2)}) %copy-start) | copy-done | bytes 2457624
  1.7 1.5 %fusion = bf16[12,32,128]{2,0,1:T(8,128)(2,1)S(1)} fusion(bf16[32,300,128]{2,0,1:T(8,128)(2,1)S(1)} %copy-done, bf16[12,300]{1,0:T(8,128)(2,1)} %param.24), kind=kOutput, calls=%fused_computation | convolution fusion | flops 29491200 | bytes 2563104 | tf_op jit(solution)/shard_map/ks,psc->kpc/dot_general | solution.py:509
  3.2 0.0 copy-done.3
  3.2 0.0 copy-done.2
  3.2 0.0 copy-start.1
  3.3 1.9 %copy-done.1 = f32[12,32,16,128]{3,2,1,0:T(8,128)S(1)} copy-done((f32[12,32,16,128]{3,2,1,0:T(8,128)S(1)}, f32[12,32,16,128]{3,2,1,0:T(8,128)}, u32[]{:S(2)}) %copy-start.1) | copy-done | bytes 3145752
  5.1 0.7 %shard_map.137 = (f32[12,16,128]{2,1,0:T(8,128)S(1)}, f32[12,16,128]{2,1,0:T(8,128)S(1)}, f32[13,16,128]{2,1,0:T(8,128)S(1)}, f32[13,48,128]{2,1,0:T(8,128)S(1)}...) custom-call(s32[1,32]{1,0:T(1,128)S(1)} %bitcast.9, s32[1,32]{1,0:T(1,128)S(1)} %bitcast.10, ...), custom_call_target="tpu_custom_call" | custom-call | tf_op jit(solution)/shard_map/pallas_call | solution.py:515
  5.8 3.4 %collective-permute-start = (f32[12,16,128]{2,1,0:T(8,128)S(1)}, f32[12,16,128]{2,1,0:T(8,128)S(1)}, u32[]{:S(2)}, u32[]{:S(2)}) collective-permute-start(f32[12,16,128]{2,1,0:T(8,128)S(1)} %get-tuple-element.11), channel_id=1, source_target_pairs={{0,4},{4,8},{8,12},{12,16},{16,20},{20,24},{24,28},{1,5},{5,9},{9,... | collective-permute-start | bytes 294920 | tf_op jit(solution)/shard_map/ppermute | solution.py:528
  9.3 3.3 %collective-permute-start.1 = (f32[12,16,128]{2,1,0:T(8,128)S(1)}, f32[12,16,128]{2,1,0:T(8,128)S(1)}, u32[]{:S(2)}, u32[]{:S(2)}) collective-permute-start(f32[12,16,128]{2,1,0:T(8,128)S(1)} %get-tuple-element.12), channel_id=1, source_target_pairs={{4,0},{8,4},{12,8},{16,12},{20,16},{24,20},{28,24},{5,1},{9,5},{13... | collective-permute-start | bytes 294920 | tf_op jit(solution)/shard_map/ppermute | solution.py:529
  12.6 1.6 %collective-permute-start.4 = (f32[13,16,128]{2,1,0:T(8,128)S(1)}, f32[13,16,128]{2,1,0:T(8,128)S(1)}, u32[]{:S(2)}, u32[]{:S(2)}) collective-permute-start(f32[13,16,128]{2,1,0:T(8,128)S(1)} %get-tuple-element.16), channel_id=1, source_target_pairs={{0,2},{1,3},{2,0},{3,1},{4,6},{5,7},{6,4},{7,5},{8,10},{9,11},{10,... | collective-permute-start | bytes 319496 | tf_op jit(solution)/shard_map/ppermute | solution.py:531
  14.2 0.0 collective-permute-start.2
  14.2 1.7 %collective-permute-start.3 = (f32[13,48,128]{2,1,0:T(8,128)S(1)}, f32[13,48,128]{2,1,0:T(8,128)S(1)}, u32[]{:S(2)}, u32[]{:S(2)}) collective-permute-start(f32[13,48,128]{2,1,0:T(8,128)S(1)} %get-tuple-element.15), channel_id=1, source_target_pairs={{0,3},{1,0},{2,1},{3,2},{4,7},{5,4},{6,5},{7,6},{8,11},{9,8},{10,9... | collective-permute-start | bytes 958472 | tf_op jit(solution)/shard_map/ppermute | solution.py:531
  15.9 0.0 copy-done.9
  15.9 0.0 copy-done.7
  15.9 0.0 copy-done.12
  15.9 0.0 copy-done.11
  15.9 0.0 copy-done.10
  15.9 0.0 copy-done.8
  15.9 0.0 copy-start.4
  16.0 0.0 copy-start.5
  16.0 0.0 copy-start.6
  16.0 13.6 %shard_map.136.chem_in = f32[12,16,16,128]{3,2,1,0:T(8,128)S(1)} custom-call(f32[12,32,16,128]{3,2,1,0:T(8,128)S(1)} %copy-done.1, bf16[12,256]{1,0:T(8,128)(2,1)S(1)} %bitcast.11, f32[1,256]{1,0:T(1,128)S(1)} %bitcast.13, bf16[256,256]{1,0:T(8,128)(2,1)S(1)} %copy-done.7, f32[1,256]{1,0:T(1,128)S(1)} %bitcast.15, bf16[12,256]{1,0:T(8,128)(2,1)S(1)} %copy-done.9, ...), custom_call_target="tpu_custom_call" | custom-call | flops 4697620480 | bytes 3145728 | tf_op jit(solution)/shard_map/pallas_call | solution.py:552
  29.6 0.0 collective-permute-done.from_low_x
  29.6 0.0 collective-permute-done.1.from_high_x
  29.6 0.0 collective-permute-done.4.refs_3_
  29.6 0.0 collective-permute-done.2.refs_1_
  29.6 0.0 collective-permute-done.3.refs_2_
  29.6 0.0 copy-done.4
  29.7 0.0 copy-done.5
  29.7 0.0 copy-done.6
  29.7 18.4 %shard_map.138 = f32[12,32,16,128]{3,2,1,0:T(8,128)} custom-call(f32[12,32,16,128]{3,2,1,0:T(8,128)S(1)} %copy-done.1, f32[12,32,16,128]{3,2,1,0:T(8,128)S(1)} %copy-done.4, f32[3,32,16,128]{3,2,1,0:T(8,128)S(1)} %copy-done.5, f32[32,16,128]{2,1,0:T(8,128)S(1)} %copy-done.6, f32[12,16,16,128]{3,2,1,0:T(8,128)S(1)} %shard_map.136.chem_in, ...), custom_call_target="tpu_custom_call" | custom-call | flops 4697620480 | bytes 12582912 | tf_op jit(solution)/shard_map/pallas_call | solution.py:568
  (1 shorter events, 0.0 us)
Async XLA Ops:
  0.0 1.7 %copy-start = (bf16[32,300,128]{2,0,1:T(8,128)(2,1)S(1)}, bf16[32,300,128]{2,0,1:T(8,128)(2,1)}, u32[]{:S(2)}) copy-start(bf16[32,300,128]{2,0,1:T(8,128)(2,1)} %param.25) | copy-start | bytes 7372804
  0.0 3.2 %copy-start.3 = (s32[32]{0:T(128)S(1)}, s32[32]{0:T(128)}, u32[]{:S(2)}) copy-start(s32[32]{0:T(128)} %param.27) | copy-start | bytes 388
  0.0 3.2 %copy-start.2 = (s32[32,1]{0,1:T(1,128)S(1)}, s32[32,1]{0,1:T(1,128)}, u32[]{:S(2)}) copy-start(s32[32,1]{0,1:T(1,128)} %param.26) | copy-start | bytes 388
  0.0 15.9 %copy-start.9 = (bf16[12,256]{1,0:T(8,128)(2,1)S(1)}, bf16[12,256]{1,0:T(8,128)(2,1)}, u32[]{:S(2)}) copy-start(bf16[12,256]{1,0:T(8,128)(2,1)} %refs_8_.1) | copy-start | bytes 18436
  0.0 15.9 %copy-start.7 = (bf16[256,256]{1,0:T(8,128)(2,1)S(1)}, bf16[256,256]{1,0:T(8,128)(2,1)}, u32[]{:S(2)}) copy-start(bf16[256,256]{1,0:T(8,128)(2,1)} %refs_6_.1) | copy-start | bytes 393220
  0.0 15.9 %copy-start.12 = (f32[12]{0:T(128)S(1)}, f32[12]{0:T(128)}, u32[]{:S(2)}) copy-start(f32[12]{0:T(128)} %param.23) | copy-start | bytes 148
  0.0 15.9 %copy-start.11 = (f32[256]{0:T(256)S(1)}, f32[256]{0:T(256)}, u32[]{:S(2)}) copy-start(f32[256]{0:T(256)} %param.21) | copy-start | bytes 3076
  0.1 15.9 %copy-start.10 = (f32[256]{0:T(256)S(1)}, f32[256]{0:T(256)}, u32[]{:S(2)}) copy-start(f32[256]{0:T(256)} %param.19) | copy-start | bytes 3076
  0.1 15.9 %copy-start.8 = (bf16[256,12]{0,1:T(8,128)(2,1)S(1)}, bf16[256,12]{0,1:T(8,128)(2,1)}, u32[]{:S(2)}) copy-start(bf16[256,12]{0,1:T(8,128)(2,1)} %param.18) | copy-start | bytes 18436
  3.2 1.9 %copy-start.1 = (f32[12,32,16,128]{3,2,1,0:T(8,128)S(1)}, f32[12,32,16,128]{3,2,1,0:T(8,128)}, u32[]{:S(2)}) copy-start(f32[12,32,16,128]{3,2,1,0:T(8,128)} %section.5) | copy-start | bytes 9437188
  5.8 23.7 %collective-permute-start = (f32[12,16,128]{2,1,0:T(8,128)S(1)}, f32[12,16,128]{2,1,0:T(8,128)S(1)}, u32[]{:S(2)}, u32[]{:S(2)}) collective-permute-start(f32[12,16,128]{2,1,0:T(8,128)S(1)} %get-tuple-element.11), channel_id=1, source_target_pairs={{0,4},{4,8},{8,12},{12,16},{16,20},{20,24},{24,28},{1,5},{5,9},{9,... | collective-permute-start | bytes 294920 | tf_op jit(solution)/shard_map/ppermute | solution.py:528
  9.3 20.3 %collective-permute-start.1 = (f32[12,16,128]{2,1,0:T(8,128)S(1)}, f32[12,16,128]{2,1,0:T(8,128)S(1)}, u32[]{:S(2)}, u32[]{:S(2)}) collective-permute-start(f32[12,16,128]{2,1,0:T(8,128)S(1)} %get-tuple-element.12), channel_id=1, source_target_pairs={{4,0},{8,4},{12,8},{16,12},{20,16},{24,20},{28,24},{5,1},{9,5},{13... | collective-permute-start | bytes 294920 | tf_op jit(solution)/shard_map/ppermute | solution.py:529
  12.6 17.0 %collective-permute-start.4 = (f32[13,16,128]{2,1,0:T(8,128)S(1)}, f32[13,16,128]{2,1,0:T(8,128)S(1)}, u32[]{:S(2)}, u32[]{:S(2)}) collective-permute-start(f32[13,16,128]{2,1,0:T(8,128)S(1)} %get-tuple-element.16), channel_id=1, source_target_pairs={{0,2},{1,3},{2,0},{3,1},{4,6},{5,7},{6,4},{7,5},{8,10},{9,11},{10,... | collective-permute-start | bytes 319496 | tf_op jit(solution)/shard_map/ppermute | solution.py:531
  14.2 15.5 %collective-permute-start.2 = (f32[13,48,128]{2,1,0:T(8,128)S(1)}, f32[13,48,128]{2,1,0:T(8,128)S(1)}, u32[]{:S(2)}, u32[]{:S(2)}) collective-permute-start(f32[13,48,128]{2,1,0:T(8,128)S(1)} %get-tuple-element.14), channel_id=1, source_target_pairs={{0,1},{1,2},{2,3},{3,0},{4,5},{5,6},{6,7},{7,4},{8,9},{9,10},{10,1... | collective-permute-start | bytes 958472 | tf_op jit(solution)/shard_map/ppermute | solution.py:531
  14.2 15.5 %collective-permute-start.3 = (f32[13,48,128]{2,1,0:T(8,128)S(1)}, f32[13,48,128]{2,1,0:T(8,128)S(1)}, u32[]{:S(2)}, u32[]{:S(2)}) collective-permute-start(f32[13,48,128]{2,1,0:T(8,128)S(1)} %get-tuple-element.15), channel_id=1, source_target_pairs={{0,3},{1,0},{2,1},{3,2},{4,7},{5,4},{6,5},{7,6},{8,11},{9,8},{10,9... | collective-permute-start | bytes 958472 | tf_op jit(solution)/shard_map/ppermute | solution.py:531
  15.9 13.7 %copy-start.4 = (f32[12,32,16,128]{3,2,1,0:T(8,128)S(1)}, f32[12,32,16,128]{3,2,1,0:T(8,128)}, u32[]{:S(2)}) copy-start(f32[12,32,16,128]{3,2,1,0:T(8,128)} %base.1) | copy-start | bytes 9437188
  16.0 13.7 %copy-start.5 = (f32[3,32,16,128]{3,2,1,0:T(8,128)S(1)}, f32[3,32,16,128]{3,2,1,0:T(8,128)}, u32[]{:S(2)}) copy-start(f32[3,32,16,128]{3,2,1,0:T(8,128)} %velocity.1) | copy-start | bytes 2359300
  16.0 13.7 %copy-start.6 = (f32[32,16,128]{2,1,0:T(8,128)S(1)}, f32[32,16,128]{2,1,0:T(8,128)}, u32[]{:S(2)}) copy-start(f32[32,16,128]{2,1,0:T(8,128)} %diffusivity.1) | copy-start | bytes 786436
